TPU v7x, 128 devices: a whole 4x4x4 slice. The times are simulated.
128 devices in a mesh: row: 16 (over x, y_lo, core), col: 8 (over y_hi, z).
Axes of the slice: x: 4, y: 4 (y_hi: 2, y_lo: 2; y = y_hi * 2 + y_lo), z: 4, core: 2. Of those that a mesh axis runs over, the one named last changes fastest.
Arguments:
- front_init: float32 [16384, 16384], P('row', 'col'), as said below
- child_tiles: bfloat16 [4096, 256, 256], P(('row', 'col'))
- child_dest: int32 [4096], P(('row', 'col')), may hold values from 0 to 4095, as said below
Outputs:
- panel_factor: float32 [16384, 1024], P('row')
- schur_update: float32 [16384, 16384], P('row', 'col')
Inputs may be any that keep to these rules, and one draw needn't show every extreme that they name: `child_dest`: t = 64 * tile row + tile column. A tile held at col index c has its tile column in c * 8 to (c + 1) * 8 - 1. Of one device's tiles at most 4 have tile rows in one block of 4 tile rows, and in every column of the mesh one such block gets exactly 4 from every device of that column. The leading 1024 x 1024 block of front_init plus any child tiles added to it is strictly diagonally dominant.
All inputs are finite; a program needn't handle non-finite values.
Results may differ from a plain program's by a relative error of at most 0.0003.
Values may be sent and summed in bfloat16 or wider, within the bound.
A program may use at most 192 MiB of HBM per device.

v0:
```python
import jax
import jax.numpy as jnp
from jax import lax
from jax.sharding import PartitionSpec as P

PW = 1024
CAP = 4


def broadcast(array, axis, root):
    mine = lax.axis_index(axis) == root
    return lax.psum(jnp.where(mine, array, jnp.zeros_like(array)), axis)


def body(front_init, child_tiles, child_dest):
    row_count = lax.axis_size("row")
    col_count = lax.axis_size("col")
    row_extent, col_extent = front_init.shape
    tile_width = child_tiles.shape[1]
    tile_grid = col_extent * col_count // tile_width
    row_tiles = row_extent // tile_width
    col_tiles = col_extent // tile_width
    capacity = CAP
    tile_count = child_tiles.shape[0]
    col_index = lax.axis_index("col")
    tile_row = child_dest // tile_grid
    tile_col = child_dest % tile_grid
    owner_row = tile_row // row_tiles
    local_tile = (tile_row - owner_row * row_tiles) * col_tiles + (tile_col - col_index * col_tiles)
    same_owner = owner_row[:, None] == owner_row[None, :]
    positions = jnp.arange(tile_count)
    earlier = positions[None, :] < positions[:, None]
    send_rank = jnp.sum((same_owner & earlier).astype(jnp.int32), axis=1)
    send_slot = owner_row * capacity + send_rank
    outgoing = (
        jnp.zeros((row_count * capacity, tile_width, tile_width), jnp.bfloat16)
        .at[send_slot]
        .set(child_tiles)
    )
    targets = jnp.full((row_count * capacity,), -1, jnp.int32).at[send_slot].set(local_tile)
    arrived, places = (
        lax.all_to_all(outgoing, "row", split_axis=0, concat_axis=0, tiled=True),
        lax.all_to_all(targets, "row", split_axis=0, concat_axis=0, tiled=True),
    )
    onehot = (places[None, :] == jnp.arange(row_tiles * col_tiles)[:, None]).astype(jnp.bfloat16)
    summed = jnp.dot(
        onehot,
        arrived.reshape(arrived.shape[0], tile_width * tile_width),
        preferred_element_type=jnp.float32,
    )
    added_tiles = (
        summed.reshape(row_tiles, col_tiles, tile_width, tile_width)
        .transpose(0, 2, 1, 3)
        .reshape(row_extent, col_extent)
    )
    front_sum = front_init + added_tiles
    column_panel = broadcast(front_sum[:, :PW], "col", 0)
    pivot_raw = broadcast(column_panel, "row", 0)
    pivot_sym = (pivot_raw + pivot_raw.T) * 0.5
    pivot_factor = jnp.linalg.cholesky(pivot_sym)
    row_factor = jax.scipy.linalg.solve_triangular(pivot_factor, column_panel.T, lower=True).T
    group_size = row_count // col_count
    pieces = []
    for offset in range(group_size):
        pieces.append(broadcast(row_factor, "row", group_size * col_index + offset))
    strip_factor = jnp.concatenate(pieces, axis=0)
    schur_update = front_sum - jnp.dot(
        row_factor,
        strip_factor.T,
        precision=lax.Precision.HIGHEST,
        preferred_element_type=jnp.float32,
    )
    return (row_factor, schur_update)


def solution(mesh):
    return jax.shard_map(
        body,
        mesh=mesh,
        in_specs=(P("row", "col"), P(("row", "col"), None, None), P(("row", "col"))),
        out_specs=(P("row", None), P("row", "col")),
        check_vma=False,
    )
```

profile of v0, /device:TPU:5, one launch (start us, length us, event | category | flops | bytes accessed | tf_op | source)
XLA Modules:
  0.0 1077.2 jit_solution(15334882516940550699)
XLA Ops:
  9.4 6.1 all-to-all-start
  15.6 4.2 broadcast_in_dim.9
  19.8 11.4 %scatter_fusion = bf16[64,256,256]{2,1,0:T(8,128)(2,1)} fusion(bf16[64,256,256]{2,1,0:T(8,128)(2,1)} %broadcast_in_dim.9, s32[32]{0:T(128)S(1)} %compare_select_fusion, bf16[32,256,256]{2,1,0:T(8,128)(2,1)} %param.4), kind=kCustom, calls=%fused_computation.1 | custom fusion | bytes 12583040 | tf_op jit(solution)/shard_map/scatter | solution.py:38
  31.2 5.7 all-to-all-start.1
  36.9 9.3 copy.80
  47.4 108.8 %all-to-all-done.1 = bf16[64,256,256]{2,1,0:T(8,128)(2,1)} async-done(((bf16[64,256,256]{2,1,0:T(8,128)(2,1)}), bf16[64,256,256]{2,1,0:T(8,128)(2,1)}, u32[]{:S(2)}, u32[]{:S(2)}) %all-to-all-start.1) | async-done | bytes 8388640 | tf_op jit(solution)/shard_map/all_to_all | solution.py:42
  156.2 9.4 fusion
  165.7 7.3 copy.114
  173.0 9.3 copy.110
  182.3 12.1 %add.120 = f32[1024,2048]{0,1:T(8,128)} add(f32[1024,2048]{0,1:T(8,128)} %copy.80, f32[1024,2048]{0,1:T(8,128)} %copy.110) | non-fusion elementwise | flops 2097152 | bytes 25165824 | tf_op jit(solution)/shard_map/add | solution.py:56
  194.4 5.0 slice_select_fusion
  199.5 125.5 %all-reduce.6.cloned.1.call-done = f32[1024,1024]{0,1:T(8,128)} async-done(((f32[1024,1024]{0,1:T(8,128)}), f32[1024,1024]{0,1:T(8,128)}) %all-reduce.6.cloned.1.call-update) | async-done | bytes 4194320 | tf_op jit(solution)/shard_map/psum | solution.py:12
  325.0 2.8 broadcast_select_fusion.2
  327.9 122.2 %all-reduce.8.cloned.1.call-done = f32[1024,1024]{0,1:T(8,128)} async-done(((f32[1024,1024]{0,1:T(8,128)}), f32[1024,1024]{0,1:T(8,128)}) %all-reduce.8.cloned.1.call-update) | async-done | bytes 4194320 | tf_op jit(solution)/shard_map/psum | solution.py:12
  450.2 5.3 copy.81
  455.5 6.9 fusion.7
  462.4 13.8 %copy.82 = f32[1024,1024]{0,1:T(8,128)} copy(f32[1024,1024]{1,0:T(8,128)} %fusion.7) | data formatting | bytes 8388608 | tf_op jit(solution)/shard_map/mul | solution.py:59
  476.2 4.4 fusion.6
  480.7 2.0 copy-done.3
  482.7 11.7 %cholesky.222 = f32[128,128]{1,0:T(8,128)S(1)} custom-call(f32[128,128]{1,0:T(8,128)S(1)} %cholesky.577), custom_call_target="Cholesky" | custom-call | tf_op jit(solution)/shard_map/jit(cholesky)/cholesky | solution.py:60
  494.5 9.8 custom-call.63
  507.7 11.7 %cholesky.243 = f32[128,128]{1,0:T(8,128)S(1)} custom-call(f32[128,128]{1,0:T(8,128)S(1)} %cholesky.581), custom_call_target="Cholesky" | custom-call | tf_op jit(solution)/shard_map/jit(cholesky)/cholesky | solution.py:60
  519.7 9.8 custom-call.64
  530.7 2.0 copy-done
  532.6 2.4 convolution_subtract_fusion.6
  535.1 11.7 %cholesky.466 = f32[128,128]{1,0:T(8,128)S(1)} custom-call(f32[128,128]{1,0:T(8,128)S(1)} %cholesky.586), custom_call_target="Cholesky" | custom-call | tf_op jit(solution)/shard_map/jit(cholesky)/cholesky | solution.py:60
  547.6 9.8 custom-call.65
  558.6 3.5 convolution_subtract_fusion.7
  562.2 11.7 %cholesky.485 = f32[128,128]{1,0:T(8,128)S(1)} custom-call(f32[128,128]{1,0:T(8,128)S(1)} %cholesky.591), custom_call_target="Cholesky" | custom-call | tf_op jit(solution)/shard_map/jit(cholesky)/cholesky | solution.py:60
  574.7 9.8 custom-call.66
  585.6 3.1 convolution_subtract_fusion.8
  588.8 11.9 %cholesky.504 = f32[128,128]{1,0:T(8,128)S(1)} custom-call(f32[128,128]{1,0:T(8,128)S(1)} %cholesky.596), custom_call_target="Cholesky" | custom-call | tf_op jit(solution)/shard_map/jit(cholesky)/cholesky | solution.py:60
  601.4 9.8 custom-call.67
  612.3 3.1 convolution_subtract_fusion.9
  615.4 11.7 %cholesky.524 = f32[128,128]{1,0:T(8,128)S(1)} custom-call(f32[128,128]{1,0:T(8,128)S(1)} %cholesky.601), custom_call_target="Cholesky" | custom-call | tf_op jit(solution)/shard_map/jit(cholesky)/cholesky | solution.py:60
  627.9 9.8 custom-call.68
  638.7 3.1 convolution_subtract_fusion.10
  641.8 11.7 %cholesky.544 = f32[128,128]{1,0:T(8,128)S(1)} custom-call(f32[128,128]{1,0:T(8,128)S(1)} %cholesky.606), custom_call_target="Cholesky" | custom-call | tf_op jit(solution)/shard_map/jit(cholesky)/cholesky | solution.py:60
  654.3 9.8 custom-call.69
  665.0 2.1 convolution_subtract_fusion.11
  667.1 11.7 %cholesky.562 = f32[128,128]{1,0:T(8,128)S(1)} custom-call(f32[128,128]{1,0:T(8,128)S(1)} %convolution_subtract_fusion.11), custom_call_target="Cholesky" | custom-call | tf_op jit(solution)/shard_map/jit(cholesky)/cholesky | solution.py:60
  689.0 4.9 select_select_fusion
  693.9 23.7 %while.1 = (s32[]{:T(128)}, f32[1024,1024]{0,1:T(8,128)}, s32[8,2]{0,1:T(2,128)S(1)}, f32[8,128,128]{2,1,0:T(8,128)S(1)}, s32[]{:T(128)}) while((s32[]{:T(128)}, f32[1024,1024]{0,1:T(8,128)}, s32[8,2]{0,1:T(2,128)S(1)}, f32[8,128,128]{2,1,0:T(8,128)S(1)}, s32[]{:T(128)}) %tuple.63), condition=%wide.while_cond, body=%wide.while_body.sunk | while | flops 2 | bytes 393329 | solution.py:61
  694.5 2.2 dynamic-slice.7
  697.5 2.2 dynamic-slice.7
  700.5 2.2 dynamic-slice.7
  703.5 2.2 dynamic-slice.7
  706.5 2.2 dynamic-slice.7
  709.4 2.2 dynamic-slice.7
  712.4 2.2 dynamic-slice.7
  715.4 2.2 dynamic-slice.7
  717.7 78.8 %custom-call.70 = f32[8,128,128]{1,2,0:T(8,128)S(1)} custom-call(f32[8,128,128]{2,1,0:T(8,128)S(1)} %get-tuple-element.9), custom_call_target="InvertDiagBlocksLowerTriangular" | custom-call | tf_op jit(solution)/shard_map/jit(_solve_triangular)/triangular_solve | solution.py:61
  796.5 1.9 constant_dynamic-update-slice_fusion.17
  798.4 1.7 convolution_subtract_fusion.4
  803.3 2.0 fusion.25
  806.0 2.2 fusion.28
  809.0 2.6 convolution_subtract_fusion.2
  812.3 2.9 convolution_subtract_fusion.1
  815.8 3.5 convolution_subtract_fusion.3
  820.0 4.5 broadcast_select_fusion
  824.5 5.3 copy.100
  829.8 198.7 %all-reduce.10.cloned.1.call-done = (f32[1024,1024]{0,1:T(8,128)}, f32[1024,1024]{0,1:T(8,128)}) async-done(((f32[1024,1024]{0,1:T(8,128)}, f32[1024,1024]{0,1:T(8,128)}), (f32[1024,1024]{0,1:T(8,128)}, f32[1024,1024]{0,1:T(8,128)})) %all-reduce.10.cloned.1.call-update) | async-done | bytes 8388624 | tf_op jit(solution)/shard_map/psum | solution.py:12
  1028.5 32.6 %fusion.8 = f32[1024,2048]{0,1:T(8,128)} fusion(f32[1024,2048]{0,1:T(8,128)} %add.120, f32[1024,1024]{1,0:T(8,128)} %copy-done.1, f32[1024,1024]{0,1:T(8,128)} %get-tuple-element.42, f32[1024,1024]{0,1:T(8,128)} %get-tuple-element.43), kind=kOutput, calls=%fused_computation.18 | convolution fusion | flops 25773998080 | bytes 29360128 | tf_op jit(solution)/shard_map/dot_general | solution.py:67
  1061.1 9.1 copy.101
  (113 shorter events, 35.4 us)
Async XLA Ops:
  9.4 21.7 %all-to-all-start = ((s32[16,4,1]{1,2,0:T(1,128)}), s32[16,4,1]{1,2,0:T(1,128)S(1)}, u32[]{:S(2)}, u32[]{:S(2)}) async-start(s32[16,4,1]{1,2,0:T(1,128)} %bitcast), calls=%async_computation | async-start | bytes 16384 | tf_op jit(solution)/shard_map/all_to_all | solution.py:43
  31.2 125.1 %all-to-all-start.1 = ((bf16[64,256,256]{2,1,0:T(8,128)(2,1)}), bf16[64,256,256]{2,1,0:T(8,128)(2,1)}, u32[]{:S(2)}, u32[]{:S(2)}) async-start(bf16[64,256,256]{2,1,0:T(8,128)(2,1)} %scatter_fusion), calls=%async_computation.1 | async-start | bytes 16777216 | tf_op jit(solution)/shard_map/all_to_all | solution.py:42
  36.8 288.2 %all-reduce.6.cloned.1.call-start = ((), (), s32[]{:S(2)}) async-start(), calls=%async_computation.2 | async-start | bytes 8388608 | tf_op jit(solution)/shard_map/psum | solution.py:12
  199.5 250.7 %all-reduce.8.cloned.1.call-start = ((), (), s32[]{:S(2)}) async-start(), calls=%async_computation.3 | async-start | bytes 8388608 | tf_op jit(solution)/shard_map/psum | solution.py:12
  327.9 700.7 %all-reduce.10.cloned.1.call-start = ((), (), s32[]{:S(2)}) async-start(), calls=%async_computation.4 | async-start | bytes 16777216 | tf_op jit(solution)/shard_map/psum | solution.py:12
  480.7 2.0 copy-start.3
  530.7 2.0 copy-start
  796.5 4.4 copy-start.2
  819.9 4.5 copy-start.1
Sparse Core Ops, SparseCore 0:
  199.6 125.3 all-reduce.5
  328.1 122.0 all-reduce.7
  824.6 203.9 all-reduce.9
where the time goes:
time: 1090 us; the launch traced here: 1080 us
  waiting for transfers between devices  555 us (51%)
  other arithmetic  289 us (27%)
  local copies, waits for them, and re-layouts  110 us (10%)
  matrix products  91.7 us (8%)
  between operations  19.5 us (2%)
  starting transfers between devices  11.9 us (1%)
    psum x3, waiting for transfers between devices, broadcast(): return lax.psum(jnp.where(mine, array, jnp.zeros_like(array)), axis)  446 us
    another operation x30, other arithmetic, body(): pivot_factor = jnp.linalg.cholesky(pivot_sym)  168 us
    all_to_all x1, waiting for transfers between devices, body(): lax.all_to_all(outgoing, 'row', split_axis=0, concat_axis=0, tiled=True)  109 us
    another operation x3, other arithmetic, body(): jax.scipy.linalg.solve_triangular(pivot_factor, column_panel.T, lower=True)  83.7 us
    unnamed x12, local copies, waits for them, and re-layouts  35 us
    dot_general x1, matrix products, body(): jnp.dot(row_factor, strip_factor.T, precision=lax.Precision.HIGHEST, pref...  32.6 us
    another operation x14, matrix products, body(): pivot_factor = jnp.linalg.cholesky(pivot_sym)  26.3 us
    another operation x40, local copies, waits for them, and re-layouts  23.5 us
  transfers between devices with their start and end apart: 5, of which 4 were waited for; matrix products, arithmetic and copies ran while one was open for 3% of the time, Pallas kernels for 0%

commit v1 on v0

v1 whole, which is shorter than its diff:
```python
import jax
import jax.numpy as jnp
from jax import lax
from jax.experimental import pallas as pl
from jax.experimental.pallas import tpu as pltpu
from jax.sharding import PartitionSpec as P

PW = 1024
TW = 256
CAP = 4
NT = 64
ROWS = 16
COLS = 8
SLOTS = ROWS * CAP
MIB = 1024 * 1024
MESH = pl.DeviceIdType.MESH
ANY = pl.BlockSpec(memory_space=pl.ANY)

HI = lax.Precision.HIGHEST
NB = 128


def block_inverse(block):
    rows = lax.broadcasted_iota(jnp.int32, (NB, NB), 0)
    lanes = lax.broadcasted_iota(jnp.int32, (NB, NB), 1)
    left = block
    right = jnp.where(rows == lanes, 1.0, 0.0).astype(jnp.float32)
    done = []
    for group in range(NB // 8):
        height = NB - 8 * group
        row_ids = lax.broadcasted_iota(jnp.int32, (height, NB), 0)
        cols = [
            jnp.broadcast_to(left[:, 8 * group + j : 8 * group + j + 1], (height, NB))
            for j in range(8)
        ]
        scales = []
        for i in range(8):
            pivot = cols[i][i : i + 1, :]
            scales.append(lax.rsqrt(pivot))
            mult = jnp.where(row_ids > i, cols[i] * (1.0 / pivot), 0.0)
            left = left - mult * left[i : i + 1, :]
            right = right - mult * right[i : i + 1, :]
            for j in range(i + 1, 8):
                cols[j] = cols[j] - mult * cols[j][i : i + 1, :]
        done.append(right[:8] * jnp.concatenate(scales, axis=0))
        left = left[8:]
        right = right[8:]
    return jnp.concatenate(done, axis=0)


def dot_nt(a, b):
    return lax.dot_general(a, b, (((1,), (1,)), ((), ())), precision=HI, preferred_element_type=jnp.float32)


def dot_nn(a, b):
    return lax.dot_general(a, b, (((1,), (0,)), ((), ())), precision=HI, preferred_element_type=jnp.float32)


def chol_kernel(raw_ref, out_ref, a_ref, w_ref):
    n = raw_ref.shape[0]
    steps = n // NB
    step = pl.program_id(0)

    @pl.when(step == 0)
    def _():
        for i in range(steps):
            for k in range(i + 1):
                ri, rk = slice(i * NB, (i + 1) * NB), slice(k * NB, (k + 1) * NB)
                a_ref[ri, rk] = (raw_ref[ri, rk] + raw_ref[rk, ri].T) * 0.5
        w_ref[...] = jnp.zeros_like(w_ref)

    here = pl.ds(pl.multiple_of(step * NB, NB), NB)
    inv = block_inverse(a_ref[here, here])
    for j in range(steps):

        @pl.when(step == j)
        def _(j=j):
            me = slice(j * NB, (j + 1) * NB)
            w_ref[me, me] = inv
            if j > 0:
                below = dot_nn(a_ref[me, : j * NB], w_ref[: j * NB, : j * NB])
                w_ref[me, : j * NB] = -dot_nn(inv, below)
            if j + 1 < steps:
                rest = slice((j + 1) * NB, n)
                col = dot_nt(a_ref[rest, me], inv)
                a_ref[rest, me] = col
                for k in range(j + 1, steps):
                    low = col[(k - j - 1) * NB :]
                    a_ref[k * NB :, k * NB : (k + 1) * NB] -= dot_nt(low, low[:NB])
            else:
                out_ref[...] = w_ref[...]


def chol_inverse(raw):
    n = raw.shape[0]
    return pl.pallas_call(
        chol_kernel,
        grid=(n // NB,),
        out_shape=jax.ShapeDtypeStruct((n, n), jnp.float32),
        in_specs=[pl.BlockSpec((n, n), lambda i: (0, 0))],
        out_specs=pl.BlockSpec((n, n), lambda i: (0, 0)),
        scratch_shapes=[pltpu.VMEM((n, n), jnp.float32), pltpu.VMEM((n, n), jnp.float32)],
        compiler_params=pltpu.CompilerParams(vmem_limit_bytes=48 * 1024 * 1024),
        name="chol_inverse",
    )(raw)


def pack_kernel(dest_ref, tiles_ref, out_ref, target_ref, count_ref, sems):
    def clear_count(i, carry):
        count_ref[i] = 0
        return carry

    def clear_target(i, carry):
        target_ref[i] = -1
        return carry

    lax.fori_loop(0, ROWS, clear_count, 0)
    lax.fori_loop(0, SLOTS, clear_target, 0)
    count = tiles_ref.shape[0]

    def place(i, carry):
        tile = dest_ref[i]
        tile_row = tile >> 6
        owner = tile_row >> 2
        rank = count_ref[owner]
        count_ref[owner] = rank + 1
        slot = owner * CAP + rank
        target_ref[slot] = (tile_row & 3) * 8 + (tile & 7)
        pltpu.make_async_copy(tiles_ref.at[i], out_ref.at[slot], sems.at[i]).start()
        return carry

    def finish(i, carry):
        pltpu.make_async_copy(tiles_ref.at[i], out_ref.at[i], sems.at[i]).wait()
        return carry

    lax.fori_loop(0, count, place, 0)
    lax.fori_loop(0, count, finish, 0)


def pack(child_tiles, child_dest):
    count = child_tiles.shape[0]
    return pl.pallas_call(
        pack_kernel,
        out_shape=(
            jax.ShapeDtypeStruct((SLOTS, TW, TW), jnp.bfloat16),
            jax.ShapeDtypeStruct((SLOTS,), jnp.int32),
        ),
        in_specs=[pl.BlockSpec(memory_space=pltpu.SMEM), ANY],
        out_specs=(ANY, pl.BlockSpec(memory_space=pltpu.SMEM)),
        scratch_shapes=[pltpu.SMEM((ROWS,), jnp.int32), pltpu.SemaphoreType.DMA((count,))],
        name="pack",
    )(child_dest, child_tiles)


def build_lists(places_ref, head_ref, next_ref):
    def clear(i, carry):
        head_ref[i] = -1
        return carry

    lax.fori_loop(0, 32, clear, 0)

    def link(i, carry):
        slot = SLOTS - 1 - i
        tile = places_ref[slot]

        @pl.when(tile >= 0)
        def _():
            next_ref[slot] = head_ref[tile]
            head_ref[tile] = slot

        return carry

    lax.fori_loop(0, SLOTS, link, 0)


def add_children(tile, total_ref, arrived_ref, head_ref, next_ref):
    def more(slot):
        return slot >= 0

    def add(slot):
        total_ref[...] += arrived_ref[slot].astype(jnp.float32)
        return next_ref[slot]

    lax.while_loop(more, add, head_ref[tile])


def panel_kernel(places_ref, front_ref, arrived_ref, out_ref, head_ref, next_ref):
    step = pl.program_id(0)

    @pl.when(step == 0)
    def _():
        build_lists(places_ref, head_ref, next_ref)

    out_ref[...] = front_ref[...]
    add_children((step // 4) * 8 + step % 4, out_ref, arrived_ref, head_ref, next_ref)


def panel_sum(places, front_init, arrived):
    return pl.pallas_call(
        panel_kernel,
        grid=(16,),
        out_shape=jax.ShapeDtypeStruct((front_init.shape[0], PW), jnp.float32),
        in_specs=[
            pl.BlockSpec(memory_space=pltpu.SMEM),
            pl.BlockSpec((TW, TW), lambda i: (i // 4, i % 4)),
            pl.BlockSpec((SLOTS, TW, TW), lambda i: (0, 0, 0), pipeline_mode=pl.Buffered(1)),
        ],
        out_specs=pl.BlockSpec((TW, TW), lambda i: (i // 4, i % 4)),
        scratch_shapes=[pltpu.SMEM((32,), jnp.int32), pltpu.SMEM((SLOTS,), jnp.int32)],
        compiler_params=pltpu.CompilerParams(vmem_limit_bytes=24 * MIB),
        name="panel_sum",
    )(places, front_init, arrived)


def spread_kernel(
    p_ref, w_ref, prs_ref, wa_ref,
    s_pr1, r_pr1, s_ps1, r_ps1, s_w1, r_w1, s_pr2, r_pr2, s_pr3, r_pr3,
    s_ps2, r_ps2, s_ps3, r_ps3, s_w2, r_w2, s_w3, r_w3, s_w4, r_w4, local,
):
    r = lax.axis_index("row")
    c = lax.axis_index("col")
    m, k = r // 2, r % 2
    yh, z = c // 4, c % 4
    root = (r == 0) & (c == 0)

    def remote(src, dst, send, recv, dev):
        return pltpu.make_async_remote_copy(src, dst, send, recv, device_id=dev, device_id_type=MESH)

    def rows(start, size):
        return pl.ds(pl.multiple_of(start, 8), size)

    def pr1(i):
        return remote(p_ref.at[rows(128 * i, 128)], prs_ref.at[rows(128 * i, 128)], s_pr1.at[i], r_pr1.at[0], (r, i))

    def ps1(i):
        rho = k * 8 + i
        return remote(
            p_ref.at[rows(128 * i, 128)], prs_ref.at[rows(PW + 128 * rho, 128)], s_ps1.at[i], r_ps1.at[0], (rho, m)
        )

    def w1(q):
        return remote(w_ref.at[rows(8 * q, 8)], wa_ref.at[rows(8 * q, 8)], s_w1.at[q], r_w1.at[0], (q // 8, q % 8))

    own_pr = pltpu.make_async_copy(p_ref.at[pl.ds(0, 128)], prs_ref.at[pl.ds(0, 128)], local.at[0])
    own_ps = pltpu.make_async_copy(p_ref.at[pl.ds(0, 128)], prs_ref.at[pl.ds(PW, 128)], local.at[1])
    own_w = pltpu.make_async_copy(w_ref.at[pl.ds(0, 8)], wa_ref.at[pl.ds(0, 8)], local.at[2])

    def each(lo, hi, fn):
        def step(i, carry):
            fn(i)
            return carry

        lax.fori_loop(lo, hi, step, 0)

    @pl.when(c == 0)
    def _():
        own_pr.start()

        @pl.when(r == 0)
        def _():
            own_ps.start()
            own_w.start()
            each(1, ROWS * COLS, lambda q: w1(q).start())

        @pl.when(r > 0)
        def _():
            ps1(0).start()

        ps1(4).start()
        for i in range(1, 8):
            pr1(i).start()
            if i != 4:
                ps1(i).start()

    pair = (r, lax.rem(c + 4, 8))
    other_core = (2 * m + 1 - k, c)
    mine = rows(128 * c, 128)
    theirs = rows(128 * lax.rem(c + 4, 8), 128)

    def pr2():
        return remote(prs_ref.at[mine], prs_ref.at[mine], s_pr2.at[0], r_pr2.at[0], pair)

    def pr3(dz, which):
        part = (mine, theirs)[which]
        i = (dz - 1) * 2 + which
        return remote(
            prs_ref.at[part], prs_ref.at[part], s_pr3.at[i], r_pr3.at[i], (r, yh * 4 + lax.rem(z + dz, 4))
        )

    def ps_rows(o):
        return rows(PW + 128 * (2 * lax.rem(m + 8 - o, 8) + k), 128)

    def ps2(o):
        part = ps_rows(0)
        return remote(prs_ref.at[part], prs_ref.at[part], s_ps2.at[o], r_ps2.at[o], (2 * lax.rem(m + o, 8) + k, c))

    def ps3(o):
        part = ps_rows(o)
        return remote(prs_ref.at[part], prs_ref.at[part], s_ps3.at[o], r_ps3.at[o], other_core)

    def w2(o):
        part = rows(8 * (r * 8 + c), 8)
        return remote(wa_ref.at[part], wa_ref.at[part], s_w2.at[o], r_w2.at[o], (r, lax.rem(c + o, 8)))

    def w_rows(o):
        return rows(64 * (2 * lax.rem(m + 8 - o, 8) + k), 64)

    def w3(o):
        part = w_rows(0)
        return remote(wa_ref.at[part], wa_ref.at[part], s_w3.at[o], r_w3.at[o], (2 * lax.rem(m + o, 8) + k, c))

    def w4(o):
        part = w_rows(o)
        return remote(wa_ref.at[part], wa_ref.at[part], s_w4.at[o], r_w4.at[o], other_core)

    @pl.when(c > 0)
    def _():
        pr1(0).wait_recv()

    @pl.when(c == 0)
    def _():
        own_pr.wait()

    pr2().start()

    @pl.when(root)
    def _():
        own_w.wait()
        own_ps.wait()

    @pl.when(jnp.logical_not(root))
    def _():
        w1(0).wait_recv()

    each(1, 8, lambda o: w2(o).start())

    @pl.when(jnp.logical_not(root))
    def _():
        ps1(0).wait_recv()

    each(1, 8, lambda o: ps2(o).start())
    ps3(0).start()
    for dz in (1, 3, 2):
        pr3(dz, 0).start()
    pr2().wait_recv()
    for dz in (1, 3, 2):
        pr3(dz, 1).start()
    each(1, 8, lambda o: w2(o).wait_recv())
    each(1, 8, lambda o: w3(o).start())
    w4(0).start()

    def forward_w(o):
        w3(o).wait_recv()
        w4(o).start()

    each(1, 8, forward_w)

    def forward_ps(o):
        ps2(o).wait_recv()
        ps3(o).start()

    each(1, 8, forward_ps)

    @pl.when(c == 0)
    def _():
        @pl.when(r == 0)
        def _():
            each(1, ROWS * COLS, lambda q: w1(q).wait_send())

        @pl.when(r > 0)
        def _():
            ps1(0).wait_send()

        for i in range(1, 8):
            pr1(i).wait_send()
            ps1(i).wait_send()

    pr2().wait_send()
    for dz in (1, 2, 3):
        for which in (0, 1):
            pr3(dz, which).wait()

    def finish(o):
        w2(o).wait_send()
        w3(o).wait_send()
        ps2(o).wait_send()

    each(1, 8, finish)

    def finish_core(o):
        ps3(o).wait()
        w4(o).wait()

    each(0, 8, finish_core)


def spread(panel, inverse):
    dma = pltpu.SemaphoreType.DMA
    sizes = [8, 1, 8, 1, 128, 1, 1, 1, 6, 6, 8, 8, 8, 8, 8, 8, 8, 8, 8, 8, 3]
    return pl.pallas_call(
        spread_kernel,
        out_shape=(
            jax.ShapeDtypeStruct((3 * PW, PW), jnp.float32),
            jax.ShapeDtypeStruct((PW, PW), jnp.float32),
        ),
        in_specs=[ANY, ANY],
        out_specs=(ANY, ANY),
        scratch_shapes=[dma((size,)) for size in sizes],
        compiler_params=pltpu.CompilerParams(has_side_effects=True),
        name="spread",
    )(panel, inverse)


def split(x):
    high = x.astype(jnp.bfloat16)
    return high, (x - high.astype(jnp.float32)).astype(jnp.bfloat16)


def dot3(ah, al, bh, bl):
    def nt(a, b):
        return lax.dot_general(a, b, (((1,), (1,)), ((), ())), preferred_element_type=jnp.float32)

    return nt(ah, bh) + (nt(ah, bl) + nt(al, bh))


def update_kernel(
    places_ref, w_ref, prs_ref, front_ref, arrived_ref, factor_ref, schur_ref,
    wh_ref, wl_ref, fh_ref, fl_ref, head_ref, next_ref,
):
    step = pl.program_id(0)

    @pl.when(step == 0)
    def _():
        build_lists(places_ref, head_ref, next_ref)
        wh_ref[...], wl_ref[...] = split(w_ref[...])

    @pl.when(step < 12)
    def _():
        ah, al = split(prs_ref[...])
        here = pl.ds(pl.multiple_of(step * TW, TW), TW)
        for j in range(PW // TW):
            out = slice(j * TW, (j + 1) * TW)
            deep = slice(0, (j + 1) * TW)
            block = dot3(ah[:, deep], al[:, deep], wh_ref[out, deep], wl_ref[out, deep])
            fh_ref[here, out], fl_ref[here, out] = split(block)

            @pl.when(step < 4)
            def _():
                factor_ref[:, out] = block

    @pl.when(step >= 12)
    def _():
        tile = step - 12
        left = pl.ds(pl.multiple_of((tile // 8) * TW, TW), TW)
        right = pl.ds(pl.multiple_of(PW + (tile % 8) * TW, TW), TW)
        schur_ref[...] = front_ref[...] - dot3(fh_ref[left, :], fl_ref[left, :], fh_ref[right, :], fl_ref[right, :])
        add_children(tile, schur_ref, arrived_ref, head_ref, next_ref)


def update(places, inverse, strips, front_init, arrived):
    def tile_map(i):
        t = jnp.maximum(i - 12, 0)
        return (t // 8, t % 8)

    return pl.pallas_call(
        update_kernel,
        grid=(44,),
        out_shape=(
            jax.ShapeDtypeStruct((PW, PW), jnp.float32),
            jax.ShapeDtypeStruct(front_init.shape, jnp.float32),
        ),
        in_specs=[
            pl.BlockSpec(memory_space=pltpu.SMEM),
            pl.BlockSpec((PW, PW), lambda i: (0, 0), pipeline_mode=pl.Buffered(1)),
            pl.BlockSpec((TW, PW), lambda i: (jnp.minimum(i, 11), 0)),
            pl.BlockSpec((TW, TW), tile_map),
            pl.BlockSpec((SLOTS, TW, TW), lambda i: (0, 0, 0), pipeline_mode=pl.Buffered(1)),
        ],
        out_specs=(
            pl.BlockSpec((TW, PW), lambda i: (jnp.minimum(i, 3), 0)),
            pl.BlockSpec((TW, TW), tile_map),
        ),
        scratch_shapes=[
            pltpu.VMEM((PW, PW), jnp.bfloat16),
            pltpu.VMEM((PW, PW), jnp.bfloat16),
            pltpu.VMEM((3 * PW, PW), jnp.bfloat16),
            pltpu.VMEM((3 * PW, PW), jnp.bfloat16),
            pltpu.SMEM((32,), jnp.int32),
            pltpu.SMEM((SLOTS,), jnp.int32),
        ],
        compiler_params=pltpu.CompilerParams(vmem_limit_bytes=52 * MIB),
        name="update",
    )(places, inverse, strips, front_init, arrived)


def body(front_init, child_tiles, child_dest):
    outgoing, targets = pack(child_tiles, child_dest)
    arrived = lax.all_to_all(outgoing, "row", split_axis=0, concat_axis=0, tiled=True)
    places = lax.all_to_all(targets, "row", split_axis=0, concat_axis=0, tiled=True)
    panel = panel_sum(places, front_init, arrived)
    inverse = chol_inverse(panel)
    strips, inverse_all = spread(panel, inverse)
    return update(places, inverse_all, strips, front_init, arrived)


def solution(mesh):
    return jax.shard_map(
        body,
        mesh=mesh,
        in_specs=(P("row", "col"), P(("row", "col"), None, None), P(("row", "col"))),
        out_specs=(P("row", None), P("row", "col")),
        check_vma=False,
    )
```

time: 1090 us -> 658 us (0.60)
  Pallas kernels: 0 us -> 504 us
  waiting for transfers between devices: 555 us -> 118 us
  other arithmetic: 289 us -> 0.67 us
  local copies, waits for them, and re-layouts: 110 us -> 8.73 us
  matrix products: 91.7 us -> 0 us
  between operations: 19.5 us -> 0.69 us
    pallas_call x0 -> x5, Pallas kernels: none -> 504 us  [the longest x1 246 us: spread(): pl.pallas_call(spread_kernel, out_shape=(jax.ShapeDtypeStruct((3 * PW, PW...]
    psum x3 -> x0, waiting for transfers between devices: 446 us -> none  [broadcast(): return lax.psum(jnp.where(mine, array, jnp.zeros_like(array)), axis)]
    another operation x33 -> x0, other arithmetic: 251 us -> none  [the longest x30 168 us: body(): pivot_factor = jnp.linalg.cholesky(pivot_sym)]
    another operation x29 -> x0, matrix products: 49.7 us -> none  [the longest x14 26.3 us: body(): pivot_factor = jnp.linalg.cholesky(pivot_sym)]
    dot_general x2 -> x0, matrix products: 42 us -> none  [the longest x1 32.6 us: body(): jnp.dot(row_factor, strip_factor.T, precision=lax.Precision.HIGHEST, pref...]
    another operation x66 -> x0, local copies, waits for them, and re-layouts: 28.9 us -> none
    unnamed x12 -> x6, local copies, waits for them, and re-layouts: 35 us -> 7.4 us
    mul x1 -> x0, local copies, waits for them, and re-layouts: 13.8 us -> none  [body(): pivot_sym = (pivot_raw + pivot_raw.T) * 0.5]
  transfers between devices with their start and end apart: 5 -> 1, of which waited for: 4 -> 1; matrix products, arithmetic and copies ran while one was open for 3% -> 0% of each run, Pallas kernels for 0% -> 0%
where the time goes in v1:
time: 658 us; the launch traced here: 649 us
  Pallas kernels  504 us (77%)
  waiting for transfers between devices  118 us (18%)
  blocking collectives  9.43 us (1%)
  local copies, waits for them, and re-layouts  8.73 us (1%)
  starting transfers between devices  7.2 us (1%)
    pallas_call x1, Pallas kernels, spread(): pl.pallas_call(spread_kernel, out_shape=(jax.ShapeDtypeStruct((3 * PW, PW...  246 us
    pallas_call x1, Pallas kernels, pack(): pl.pallas_call(pack_kernel, out_shape=(jax.ShapeDtypeStruct((SLOTS, TW, T...  130 us
    all_to_all x1, waiting for transfers between devices, body(): lax.all_to_all(outgoing, 'row', split_axis=0, concat_axis=0, tiled=True)  118 us
    pallas_call x1, Pallas kernels, update(): pl.pallas_call(update_kernel, grid=(44,), out_shape=(jax.ShapeDtypeStruct...  69.8 us
    pallas_call x1, Pallas kernels, chol_inverse(): pl.pallas_call(chol_kernel, grid=(n // NB,), out_shape=jax.ShapeDtypeStru...  52.6 us
  transfers between devices with their start and end apart: 1, of which 1 were waited for; matrix products, arithmetic and copies ran while one was open for 0% of the time, Pallas kernels for 0%

profile of v1, /device:TPU:5, one launch (start us, length us, event | category | flops | bytes accessed | tf_op | source)
XLA Modules:
  0.0 649.3 jit_solution(16033210888199876901)
XLA Ops:
  0.6 130.1 %pack.1 = (bf16[64,256,256]{2,1,0:T(8,128)(2,1)}, s32[64]{0:T(128)}) custom-call(s32[32]{0:T(128)} %dest_ref.1, bf16[32,256,256]{2,1,0:T(8,128)(2,1)} %tiles_ref.1), custom_call_target="tpu_custom_call" | custom-call | tf_op jit(solution)/shard_map/pack/pallas_call | solution.py:142
  130.8 0.7 all_to_all.10
  131.5 9.4 %all_to_all.16 = s32[16,4,1]{1,2,0:T(1,128)S(1)} all-to-all(s32[16,4,1]{1,2,0:T(1,128)S(1)} %bitcast.2), channel_id=1, replica_groups=mesh['row'=16,'col'=8] {'row'}, dimensions={0} | all-to-all | bytes 512 | tf_op jit(solution)/shard_map/all_to_all | solution.py:499
  140.9 7.2 %all-to-all-start.1 = ((bf16[64,256,256]{2,1,0:T(8,128)(2,1)}), bf16[64,256,256]{2,1,0:T(8,128)(2,1)}, u32[]{:S(2)}, u32[]{:S(2)}) async-start(bf16[64,256,256]{2,1,0:T(8,128)(2,1)} %get-tuple-element.7), calls=%async_computation.1 | async-start | bytes 16777216 | tf_op jit(solution)/shard_map/all_to_all | solution.py:498
  148.1 0.5 broadcast.3
  148.6 0.7 reduce.3
  149.3 0.1 all_to_all.12.places_ref
  149.4 118.1 %all-to-all-done.1.arrived_ref = bf16[64,256,256]{2,1,0:T(8,128)(2,1)} async-done(((bf16[64,256,256]{2,1,0:T(8,128)(2,1)}), bf16[64,256,256]{2,1,0:T(8,128)(2,1)}, u32[]{:S(2)}, u32[]{:S(2)}) %all-to-all-start.1) | async-done | bytes 8388640 | tf_op jit(solution)/shard_map/all_to_all | solution.py:498
  267.5 0.0 copy-start.1
  267.5 3.4 copy-done.1
  270.9 6.5 panel_sum.1.raw_ref.p_ref
  277.4 0.0 copy-start
  277.4 2.0 copy-done
  279.4 52.6 %chol_inverse.1.w_ref = f32[1024,1024]{1,0:T(8,128)S(1)} custom-call(f32[1024,1024]{1,0:T(8,128)} %copy-done), custom_call_target="tpu_custom_call" | custom-call | tf_op jit(solution)/shard_map/chol_inverse/pallas_call | solution.py:96
  332.0 0.0 copy-start.2
  332.0 2.0 copy-done.2
  334.0 245.6 %spread.1 = (f32[3072,1024]{1,0:T(8,128)}, f32[1024,1024]{1,0:T(8,128)}) custom-call(f32[1024,1024]{1,0:T(8,128)} %copy-done, f32[1024,1024]{1,0:T(8,128)} %copy-done.2), custom_call_target="tpu_custom_call" | custom-call | tf_op jit(solution)/shard_map/spread/pallas_call | solution.py:400
  579.6 69.8 %update.1 = (f32[1024,1024]{1,0:T(8,128)}, f32[1024,2048]{1,0:T(8,128)}) custom-call(s32[64]{0:T(128)S(1)} %all_to_all.12.places_ref, f32[1024,1024]{1,0:T(8,128)} %get-tuple-element.8.w_ref, f32[3072,1024]{1,0:T(8,128)} %get-tuple-element.9.prs_ref, f32[1024,2048]{1,0:T(8,128)} %front_ref.3, bf16[64,256,256]{2,1,0:T(8,128)(2,1)} %all-to-all-done.1.arrived_ref), custom_call_target="tpu_custom_call" | custom-call | tf_op jit(solution)/shard_map/update/pallas_call | solution.py:465
Async XLA Ops:
  140.9 126.6 %all-to-all-start.1 = ((bf16[64,256,256]{2,1,0:T(8,128)(2,1)}), bf16[64,256,256]{2,1,0:T(8,128)(2,1)}, u32[]{:S(2)}, u32[]{:S(2)}) async-start(bf16[64,256,256]{2,1,0:T(8,128)(2,1)} %get-tuple-element.7), calls=%async_computation.1 | async-start | bytes 16777216 | tf_op jit(solution)/shard_map/all_to_all | solution.py:498
  267.5 3.4 copy-start.1
  277.4 2.0 copy-start
  332.0 2.0 copy-start.2

commit v2 on v1

v2 whole, which is shorter than its diff:
```python
import jax
import jax.numpy as jnp
from jax import lax
from jax.experimental import pallas as pl
from jax.experimental.pallas import tpu as pltpu
from jax.sharding import PartitionSpec as P

PW = 1024
TW = 256
CAP = 4
NT = 64
ROWS = 16
COLS = 8
SLOTS = ROWS * CAP
MIB = 1024 * 1024
MESH = pl.DeviceIdType.MESH
ANY = pl.BlockSpec(memory_space=pl.ANY)

HI = lax.Precision.HIGHEST
NB = 128


def block_inverse(block):
    rows = lax.broadcasted_iota(jnp.int32, (NB, NB), 0)
    lanes = lax.broadcasted_iota(jnp.int32, (NB, NB), 1)
    left = block
    right = jnp.where(rows == lanes, 1.0, 0.0).astype(jnp.float32)
    done = []
    for group in range(NB // 8):
        height = NB - 8 * group
        row_ids = lax.broadcasted_iota(jnp.int32, (height, NB), 0)
        cols = [
            jnp.broadcast_to(left[:, 8 * group + j : 8 * group + j + 1], (height, NB))
            for j in range(8)
        ]
        scales = []
        for i in range(8):
            pivot = cols[i][i : i + 1, :]
            scales.append(lax.rsqrt(pivot))
            mult = jnp.where(row_ids > i, cols[i] * (1.0 / pivot), 0.0)
            left = left - mult * left[i : i + 1, :]
            right = right - mult * right[i : i + 1, :]
            for j in range(i + 1, 8):
                cols[j] = cols[j] - mult * cols[j][i : i + 1, :]
        done.append(right[:8] * jnp.concatenate(scales, axis=0))
        left = left[8:]
        right = right[8:]
    return jnp.concatenate(done, axis=0)


def dot_nt(a, b):
    return lax.dot_general(a, b, (((1,), (1,)), ((), ())), precision=HI, preferred_element_type=jnp.float32)


def dot_nn(a, b):
    return lax.dot_general(a, b, (((1,), (0,)), ((), ())), precision=HI, preferred_element_type=jnp.float32)


def symmetrise(raw_ref, a_ref):
    for i in range(PW // NB):
        for k in range(i + 1):
            ri, rk = slice(i * NB, (i + 1) * NB), slice(k * NB, (k + 1) * NB)
            a_ref[ri, rk] = (raw_ref[ri, rk] + raw_ref[rk, ri].T) * 0.5


def chol_inverse(a_ref, w_ref):
    n = a_ref.shape[0]
    steps = n // NB
    w_ref[...] = jnp.zeros_like(w_ref)

    def run(step, carry):
        here = pl.ds(pl.multiple_of(step * NB, NB), NB)
        inv = block_inverse(a_ref[here, here])
        for j in range(steps):

            @pl.when(step == j)
            def _(j=j):
                me = slice(j * NB, (j + 1) * NB)
                w_ref[me, me] = inv
                if j > 0:
                    below = dot_nn(a_ref[me, : j * NB], w_ref[: j * NB, : j * NB])
                    w_ref[me, : j * NB] = -dot_nn(inv, below)
                if j + 1 < steps:
                    rest = slice((j + 1) * NB, n)
                    col = dot_nt(a_ref[rest, me], inv)
                    a_ref[rest, me] = col
                    for k in range(j + 1, steps):
                        low = col[(k - j - 1) * NB :]
                        a_ref[k * NB :, k * NB : (k + 1) * NB] -= dot_nt(low, low[:NB])

        return carry

    lax.fori_loop(0, steps, run, 0)


def pack_kernel(dest_ref, tiles_ref, out_ref, target_ref, count_ref, sems):
    def clear_count(i, carry):
        count_ref[i] = 0
        return carry

    def clear_target(i, carry):
        target_ref[i] = -1
        return carry

    lax.fori_loop(0, ROWS, clear_count, 0)
    lax.fori_loop(0, SLOTS, clear_target, 0)
    count = tiles_ref.shape[0]

    def place(i, carry):
        tile = dest_ref[i]
        tile_row = tile >> 6
        owner = tile_row >> 2
        rank = count_ref[owner]
        count_ref[owner] = rank + 1
        slot = owner * CAP + rank
        target_ref[slot] = (tile_row & 3) * 8 + (tile & 7)
        pltpu.make_async_copy(tiles_ref.at[i], out_ref.at[slot], sems.at[i]).start()
        return carry

    def finish(i, carry):
        pltpu.make_async_copy(tiles_ref.at[i], out_ref.at[i], sems.at[i]).wait()
        return carry

    lax.fori_loop(0, count, place, 0)
    lax.fori_loop(0, count, finish, 0)


def pack(child_tiles, child_dest):
    count = child_tiles.shape[0]
    return pl.pallas_call(
        pack_kernel,
        out_shape=(
            jax.ShapeDtypeStruct((SLOTS, TW, TW), jnp.bfloat16),
            jax.ShapeDtypeStruct((SLOTS,), jnp.int32),
        ),
        in_specs=[pl.BlockSpec(memory_space=pltpu.SMEM), pl.BlockSpec(memory_space=pltpu.VMEM)],
        out_specs=(ANY, pl.BlockSpec(memory_space=pltpu.SMEM)),
        scratch_shapes=[pltpu.SMEM((ROWS,), jnp.int32), pltpu.SemaphoreType.DMA((count,))],
        compiler_params=pltpu.CompilerParams(vmem_limit_bytes=16 * MIB),
        name="pack",
    )(child_dest, child_tiles)


def build_lists(places_ref, head_ref, next_ref):
    def clear(i, carry):
        head_ref[i] = -1
        return carry

    lax.fori_loop(0, 32, clear, 0)

    def link(i, carry):
        slot = SLOTS - 1 - i
        tile = places_ref[slot]

        @pl.when(tile >= 0)
        def _():
            next_ref[slot] = head_ref[tile]
            head_ref[tile] = slot

        return carry

    lax.fori_loop(0, SLOTS, link, 0)


def add_children(tile, total_ref, arrived_ref, head_ref, next_ref):
    def more(slot):
        return slot >= 0

    def add(slot):
        total_ref[...] += arrived_ref[slot].astype(jnp.float32)
        return next_ref[slot]

    lax.while_loop(more, add, head_ref[tile])


def panel_kernel(places_ref, front_ref, arrived_ref, out_ref, head_ref, next_ref):
    step = pl.program_id(0)

    @pl.when(step == 0)
    def _():
        build_lists(places_ref, head_ref, next_ref)

    out_ref[...] = front_ref[...]
    add_children((step // 4) * 8 + step % 4, out_ref, arrived_ref, head_ref, next_ref)


def panel_sum(places, front_init, arrived):
    return pl.pallas_call(
        panel_kernel,
        grid=(16,),
        out_shape=jax.ShapeDtypeStruct((front_init.shape[0], PW), jnp.float32),
        in_specs=[
            pl.BlockSpec(memory_space=pltpu.SMEM),
            pl.BlockSpec((TW, TW), lambda i: (i // 4, i % 4)),
            pl.BlockSpec((SLOTS, TW, TW), lambda i: (0, 0, 0), pipeline_mode=pl.Buffered(1)),
        ],
        out_specs=pl.BlockSpec((TW, TW), lambda i: (i // 4, i % 4)),
        scratch_shapes=[pltpu.SMEM((32,), jnp.int32), pltpu.SMEM((SLOTS,), jnp.int32)],
        compiler_params=pltpu.CompilerParams(vmem_limit_bytes=24 * MIB),
        name="panel_sum",
    )(places, front_init, arrived)


def spread_kernel(
    p_ref, prs_ref, wa_ref, a_ref, w_ref, stage_ref,
    s_pr1, r_pr1, s_swap, r_swap, s_pr2, r_pr2, s_pr3, r_pr3, s_ps2, r_ps2, s_ps3, r_ps3,
    s_w1, r_w1, s_w2, r_w2, s_w3, r_w3, s_w4, r_w4, local,
):
    r = lax.axis_index("row")
    c = lax.axis_index("col")
    m, k = r // 2, r % 2
    yh, z = c // 4, c % 4
    root = (r == 0) & (c == 0)
    pair = (r, lax.rem(c + 4, 8))
    other_core = (2 * m + 1 - k, c)

    def remote(src, dst, send, recv, dev):
        return pltpu.make_async_remote_copy(src, dst, send, recv, device_id=dev, device_id_type=MESH)

    def rows(start, size):
        return pl.ds(pl.multiple_of(start, 8), size)

    def each(lo, hi, fn):
        def step(i, carry):
            fn(i)
            return carry

        lax.fori_loop(lo, hi, step, 0)

    mine = rows(128 * c, 128)
    theirs = rows(128 * lax.rem(c + 4, 8), 128)

    def pr1(i):
        part = rows(128 * i, 128)
        return remote(p_ref.at[part], prs_ref.at[part], s_pr1.at[i], r_pr1.at[0], (r, i))

    def pr2():
        return remote(prs_ref.at[mine], prs_ref.at[mine], s_pr2.at[0], r_pr2.at[0], pair)

    def pr3(dz, which):
        part = (mine, theirs)[which]
        i = (dz - 1) * 2 + which
        return remote(
            prs_ref.at[part], prs_ref.at[part], s_pr3.at[i], r_pr3.at[i], (r, yh * 4 + lax.rem(z + dz, 4))
        )

    def swap():
        there = rows(PW + PW * k + 128 * c, 128)
        return remote(prs_ref.at[mine], prs_ref.at[there], s_swap.at[0], r_swap.at[0], (2 * c + k, m))

    def ps_rows(o):
        return rows(PW + PW * k + 128 * lax.rem(m + 8 - o, 8), 128)

    def ps2(o):
        part = ps_rows(0)
        return remote(prs_ref.at[part], prs_ref.at[part], s_ps2.at[o], r_ps2.at[o], (2 * lax.rem(m + o, 8) + k, c))

    def ps3(o):
        part = ps_rows(o)
        return remote(prs_ref.at[part], prs_ref.at[part], s_ps3.at[o], r_ps3.at[o], other_core)

    def w1(q):
        part = rows(8 * q, 8)
        return remote(w_ref.at[part], wa_ref.at[part], s_w1.at[q], r_w1.at[0], (q // 8, q % 8))

    def w2(o):
        part = rows(8 * (r * 8 + c), 8)
        return remote(wa_ref.at[part], wa_ref.at[part], s_w2.at[o], r_w2.at[o], (r, lax.rem(c + o, 8)))

    def w_rows(o):
        return rows(64 * (2 * lax.rem(m + 8 - o, 8) + k), 64)

    def w3(o):
        part = w_rows(0)
        return remote(wa_ref.at[part], wa_ref.at[part], s_w3.at[o], r_w3.at[o], (2 * lax.rem(m + o, 8) + k, c))

    def w4(o):
        part = w_rows(o)
        return remote(wa_ref.at[part], wa_ref.at[part], s_w4.at[o], r_w4.at[o], other_core)

    def move(src, dst, sem):
        copy = pltpu.make_async_copy(src, dst, sem)
        copy.start()
        copy.wait()

    @pl.when(c == 0)
    def _():
        for i in (4, 2, 6, 1, 3, 5, 7):
            pr1(i).start()
        move(p_ref.at[pl.ds(0, 128)], stage_ref, local.at[0])
        move(stage_ref, prs_ref.at[pl.ds(0, 128)], local.at[1])

    @pl.when(c > 0)
    def _():
        pr1(0).wait_recv()

    pr2().start()

    @pl.when(m == c)
    def _():
        move(prs_ref.at[mine], stage_ref, local.at[0])
        move(stage_ref, prs_ref.at[ps_rows(0)], local.at[1])

    @pl.when(m != c)
    def _():
        swap().start()

    for dz in (2, 1, 3):
        pr3(dz, 0).start()

    @pl.when(m != c)
    def _():
        swap().wait_recv()

    each(1, 8, lambda o: ps2(o).start())
    ps3(0).start()

    @pl.when(root)
    def _():
        move(p_ref, w_ref, local.at[2])
        symmetrise(w_ref, a_ref)
        chol_inverse(a_ref, w_ref)
        each(1, ROWS * COLS, lambda q: w1(q).start())
        move(w_ref.at[pl.ds(0, 8)], wa_ref.at[pl.ds(0, 8)], local.at[2])

    pr2().wait_recv()
    for dz in (2, 1, 3):
        pr3(dz, 1).start()

    @pl.when(jnp.logical_not(root))
    def _():
        w1(0).wait_recv()

    each(1, 8, lambda o: w2(o).start())
    each(1, 8, lambda o: w2(o).wait_recv())
    each(1, 8, lambda o: w3(o).start())
    w4(0).start()

    def forward_ps(o):
        ps2(o).wait_recv()
        ps3(o).start()

    each(1, 8, forward_ps)

    def forward_w(o):
        w3(o).wait_recv()
        w4(o).start()

    each(1, 8, forward_w)

    @pl.when(root)
    def _():
        each(1, ROWS * COLS, lambda q: w1(q).wait_send())

    @pl.when(c == 0)
    def _():
        each(1, 8, lambda i: pr1(i).wait_send())

    @pl.when(m != c)
    def _():
        swap().wait_send()

    pr2().wait_send()
    for dz in (1, 2, 3):
        for which in (0, 1):
            pr3(dz, which).wait()

    def finish(o):
        w2(o).wait_send()
        w3(o).wait_send()
        ps2(o).wait_send()

    each(1, 8, finish)

    def finish_core(o):
        ps3(o).wait()
        w4(o).wait()

    each(0, 8, finish_core)


def spread(panel):
    dma = pltpu.SemaphoreType.DMA
    sizes = [8, 1, 1, 1, 1, 1, 6, 6, 8, 8, 8, 8, 128, 1, 8, 8, 8, 8, 8, 8, 3]
    return pl.pallas_call(
        spread_kernel,
        out_shape=(
            jax.ShapeDtypeStruct((3 * PW, PW), jnp.float32),
            jax.ShapeDtypeStruct((PW, PW), jnp.float32),
        ),
        in_specs=[ANY],
        out_specs=(ANY, ANY),
        scratch_shapes=[
            pltpu.VMEM((PW, PW), jnp.float32),
            pltpu.VMEM((PW, PW), jnp.float32),
            pltpu.VMEM((128, PW), jnp.float32),
        ]
        + [dma((size,)) for size in sizes],
        compiler_params=pltpu.CompilerParams(has_side_effects=True, vmem_limit_bytes=40 * MIB),
        name="spread",
    )(panel)


def split(x):
    high = x.astype(jnp.bfloat16)
    return high, (x - high.astype(jnp.float32)).astype(jnp.bfloat16)


def dot3(ah, al, bh, bl):
    def nt(a, b):
        return lax.dot_general(a, b, (((1,), (1,)), ((), ())), preferred_element_type=jnp.float32)

    return nt(ah, bh) + (nt(ah, bl) + nt(al, bh))


CHUNK = 512
FILL = 3 * PW // CHUNK


def update_kernel(
    places_ref, w_ref, prs_ref, front_ref, arrived_ref, factor_ref, schur_ref,
    wh_ref, wl_ref, fh_ref, fl_ref, head_ref, next_ref,
):
    step = pl.program_id(0)

    @pl.when(step == 0)
    def _():
        build_lists(places_ref, head_ref, next_ref)
        wh_ref[...], wl_ref[...] = split(w_ref[...])

    @pl.when(step < FILL)
    def _():
        ah, al = split(prs_ref[...])
        here = pl.ds(pl.multiple_of(step * CHUNK, CHUNK), CHUNK)
        for j in range(PW // TW):
            out = slice(j * TW, (j + 1) * TW)
            deep = slice(0, (j + 1) * TW)
            block = dot3(ah[:, deep], al[:, deep], wh_ref[out, deep], wl_ref[out, deep])
            fh_ref[here, out], fl_ref[here, out] = split(block)

            @pl.when(step < PW // CHUNK)
            def _():
                factor_ref[:, out] = block

    @pl.when(step >= FILL)
    def _():
        column = step - FILL
        right = pl.ds(pl.multiple_of(PW + column * TW, TW), TW)
        schur_ref[...] = front_ref[...] - dot3(fh_ref[:PW, :], fl_ref[:PW, :], fh_ref[right, :], fl_ref[right, :])
        for i in range(PW // TW):
            total = schur_ref.at[i * TW : (i + 1) * TW, :]
            add_children(i * 8 + column, total, arrived_ref, head_ref, next_ref)


def update(places, inverse, strips, front_init, arrived):
    def column_map(i):
        return (0, jnp.maximum(i - FILL, 0))

    return pl.pallas_call(
        update_kernel,
        grid=(FILL + 8,),
        out_shape=(
            jax.ShapeDtypeStruct((PW, PW), jnp.float32),
            jax.ShapeDtypeStruct(front_init.shape, jnp.float32),
        ),
        in_specs=[
            pl.BlockSpec(memory_space=pltpu.SMEM),
            pl.BlockSpec((PW, PW), lambda i: (0, 0), pipeline_mode=pl.Buffered(1)),
            pl.BlockSpec((CHUNK, PW), lambda i: (jnp.minimum(i, FILL - 1), 0)),
            pl.BlockSpec((PW, TW), column_map),
            pl.BlockSpec((SLOTS, TW, TW), lambda i: (0, 0, 0), pipeline_mode=pl.Buffered(1)),
        ],
        out_specs=(
            pl.BlockSpec((CHUNK, PW), lambda i: (jnp.minimum(i, PW // CHUNK - 1), 0)),
            pl.BlockSpec((PW, TW), column_map),
        ),
        scratch_shapes=[
            pltpu.VMEM((PW, PW), jnp.bfloat16),
            pltpu.VMEM((PW, PW), jnp.bfloat16),
            pltpu.VMEM((3 * PW, PW), jnp.bfloat16),
            pltpu.VMEM((3 * PW, PW), jnp.bfloat16),
            pltpu.SMEM((32,), jnp.int32),
            pltpu.SMEM((SLOTS,), jnp.int32),
        ],
        compiler_params=pltpu.CompilerParams(vmem_limit_bytes=58 * MIB),
        name="update",
    )(places, inverse, strips, front_init, arrived)


def body(front_init, child_tiles, child_dest):
    outgoing, targets = pack(child_tiles, child_dest)
    arrived = lax.all_to_all(outgoing, "row", split_axis=0, concat_axis=0, tiled=True)
    places = lax.all_to_all(targets, "row", split_axis=0, concat_axis=0, tiled=True)
    panel = panel_sum(places, front_init, arrived)
    strips, inverse = spread(panel)
    return update(places, inverse, strips, front_init, arrived)


def solution(mesh):
    return jax.shard_map(
        body,
        mesh=mesh,
        in_specs=(P("row", "col"), P(("row", "col"), None, None), P(("row", "col"))),
        out_specs=(P("row", None), P("row", "col")),
        check_vma=False,
    )
```

time: 658 us -> 461 us (0.70)
  the two profiles are of different devices: /device:TPU:5 before, /device:TPU:45 now
where the time goes in v2:
time: 461 us
  Pallas kernels  298 us (65%)
  waiting for transfers between devices  132 us (29%)
  local copies, waits for them, and re-layouts  12.3 us (3%)
  blocking collectives  8.43 us (2%)
  starting transfers between devices  8.12 us (2%)
    pallas_call x1, Pallas kernels, spread(): pl.pallas_call(spread_kernel, out_shape=(jax.ShapeDtypeStruct((3 * PW, PW...  231 us
    all_to_all x1, waiting for transfers between devices, body(): lax.all_to_all(outgoing, 'row', split_axis=0, concat_axis=0, tiled=True)  132 us
    pallas_call x1, Pallas kernels, update(): pl.pallas_call(update_kernel, grid=(FILL + 8,), out_shape=(jax.ShapeDtype...  53.3 us
    unnamed x12, local copies, waits for them, and re-layouts  11.6 us
  transfers between devices with their start and end apart: 1, of which 1 were waited for; matrix products, arithmetic and copies ran while one was open for 0% of the time, Pallas kernels for 0%

profile of v2, /device:TPU:45, one launch (start us, length us, event | category | flops | bytes accessed | tf_op | source)
XLA Modules:
  0.0 460.7 jit_solution(5134789240999856716)
XLA Ops:
  0.6 0.0 copy-start.3
  0.6 2.2 copy-done.3
  2.8 0.0 copy-start.5
  2.8 0.7 copy-done.5
  3.5 8.0 %pack.1 = (bf16[64,256,256]{2,1,0:T(8,128)(2,1)S(1)}, s32[64]{0:T(128)S(1)}) custom-call(s32[32]{0:T(128)S(1)} %copy-done.5, bf16[32,256,256]{2,1,0:T(8,128)(2,1)S(1)} %copy-done.3), custom_call_target="tpu_custom_call" | custom-call | tf_op jit(solution)/shard_map/pack/pallas_call | solution.py:130
  11.5 0.0 copy-start.1
  11.5 3.4 copy-done.1
  14.9 0.1 all_to_all.10
  14.9 8.4 %all_to_all.16 = s32[16,4,1]{1,2,0:T(1,128)S(1)} all-to-all(s32[16,4,1]{1,2,0:T(1,128)S(1)} %bitcast.2), channel_id=1, replica_groups=mesh['row'=16,'col'=8] {'row'}, dimensions={0} | all-to-all | bytes 512 | tf_op jit(solution)/shard_map/all_to_all | solution.py:493
  23.4 8.1 %all-to-all-start.1 = ((bf16[64,256,256]{2,1,0:T(8,128)(2,1)}), bf16[64,256,256]{2,1,0:T(8,128)(2,1)}, u32[]{:S(2)}, u32[]{:S(2)}) async-start(bf16[64,256,256]{2,1,0:T(8,128)(2,1)} %copy-done.1), calls=%async_computation.1 | async-start | bytes 16777216 | tf_op jit(solution)/shard_map/all_to_all | solution.py:492
  31.5 0.5 broadcast.3
  32.0 0.7 reduce.3
  32.7 0.1 all_to_all.12.places_ref
  32.8 0.0 copy-start.4
  32.8 132.1 %all-to-all-done.1.arrived_ref = bf16[64,256,256]{2,1,0:T(8,128)(2,1)} async-done(((bf16[64,256,256]{2,1,0:T(8,128)(2,1)}), bf16[64,256,256]{2,1,0:T(8,128)(2,1)}, u32[]{:S(2)}, u32[]{:S(2)}) %all-to-all-start.1) | async-done | bytes 8388640 | tf_op jit(solution)/shard_map/all_to_all | solution.py:492
  164.9 0.0 copy-start
  164.9 3.4 copy-done
  168.3 6.0 %panel_sum.1.p_ref = f32[1024,1024]{1,0:T(8,128)S(1)} custom-call(s32[64]{0:T(128)S(1)} %all_to_all.12.places_ref, f32[1024,2048]{1,0:T(8,128)S(1)} %copy-done, bf16[64,256,256]{2,1,0:T(8,128)(2,1)} %all-to-all-done.1.arrived_ref), custom_call_target="tpu_custom_call" | custom-call | tf_op jit(solution)/shard_map/panel_sum/pallas_call | solution.py:188
  174.3 0.0 copy-done.4
  174.3 231.1 %spread.1 = (f32[3072,1024]{1,0:T(8,128)}, f32[1024,1024]{1,0:T(8,128)S(1)}) custom-call(f32[1024,1024]{1,0:T(8,128)S(1)} %panel_sum.1.p_ref), custom_call_target="tpu_custom_call" | custom-call | tf_op jit(solution)/shard_map/spread/pallas_call | solution.py:385
  405.4 0.0 copy-start.2
  405.4 2.0 copy-done.2
  407.4 53.3 %update.1 = (f32[1024,1024]{1,0:T(8,128)}, f32[1024,2048]{1,0:T(8,128)}) custom-call(s32[64]{0:T(128)} %copy-done.4, f32[1024,1024]{1,0:T(8,128)} %copy-done.2, f32[3072,1024]{1,0:T(8,128)} %get-tuple-element.9.prs_ref, f32[1024,2048]{1,0:T(8,128)} %front_ref.3, bf16[64,256,256]{2,1,0:T(8,128)(2,1)} %all-to-all-done.1.arrived_ref), custom_call_target="tpu_custom_call" | custom-call | tf_op jit(solution)/shard_map/update/pallas_call | solution.py:459
Async XLA Ops:
  0.6 2.2 copy-start.3
  2.8 0.7 copy-start.5
  11.5 3.4 copy-start.1
  23.4 141.5 %all-to-all-start.1 = ((bf16[64,256,256]{2,1,0:T(8,128)(2,1)}), bf16[64,256,256]{2,1,0:T(8,128)(2,1)}, u32[]{:S(2)}, u32[]{:S(2)}) async-start(bf16[64,256,256]{2,1,0:T(8,128)(2,1)} %copy-done.1), calls=%async_computation.1 | async-start | bytes 16777216 | tf_op jit(solution)/shard_map/all_to_all | solution.py:492
  32.8 141.5 %copy-start.4 = (s32[64]{0:T(128)}, s32[64]{0:T(128)S(1)}, u32[]{:S(2)}) copy-start(s32[64]{0:T(128)S(1)} %all_to_all.12.places_ref) | copy-start | bytes 772
  164.9 3.4 copy-start
  405.4 2.0 copy-start.2

commit v3 on v2

--- a/solution.py
+++ b/solution.py
@@ -63,7 +63,7 @@
             a_ref[ri, rk] = (raw_ref[ri, rk] + raw_ref[rk, ri].T) * 0.5
 
 
-def chol_inverse(a_ref, w_ref):
+def chol_inverse(a_ref, w_ref, block_done):
     n = a_ref.shape[0]
     steps = n // NB
     w_ref[...] = jnp.zeros_like(w_ref)
@@ -88,6 +88,7 @@
                         low = col[(k - j - 1) * NB :]
                         a_ref[k * NB :, k * NB : (k + 1) * NB] -= dot_nt(low, low[:NB])
 
+        block_done(step)
         return carry
 
     lax.fori_loop(0, steps, run, 0)
@@ -139,6 +140,58 @@
         compiler_params=pltpu.CompilerParams(vmem_limit_bytes=16 * MIB),
         name="pack",
     )(child_dest, child_tiles)
+
+
+PEERS = (
+    (2, 1, 0), (2, 1, 1), (1, 1, 0), (1, 1, 1), (2, 0, 0), (2, 0, 1), (3, 1, 0), (3, 1, 1),
+    (0, 1, 0), (0, 1, 1), (1, 0, 0), (1, 0, 1), (3, 0, 0), (3, 0, 1), (0, 0, 1),
+)
+
+
+def exchange_kernel(out_ref, target_ref, in_ref, place_ref, send, recv, target_send, target_recv, local):
+    r = lax.axis_index("row")
+    c = lax.axis_index("col")
+    x, y, k = r // 4, (r // 2) % 2, r % 2
+    here = pl.ds(r * CAP, CAP)
+    copies = []
+    for i, (dx, dy, dk) in enumerate(PEERS):
+        peer = lax.rem(x + dx, 4) * 4 + lax.rem(y + dy, 2) * 2 + lax.rem(k + dk, 2)
+        copies.append(
+            pltpu.make_async_remote_copy(
+                target_ref.at[peer], place_ref.at[r], target_send.at[i], target_recv.at[i],
+                device_id=(peer, c), device_id_type=MESH,
+            )
+        )
+        copies.append(
+            pltpu.make_async_remote_copy(
+                out_ref.at[pl.ds(peer * CAP, CAP)], in_ref.at[here], send.at[i], recv.at[i],
+                device_id=(peer, c), device_id_type=MESH,
+            )
+        )
+    copies.append(pltpu.make_async_copy(out_ref.at[here], in_ref.at[here], local.at[0]))
+    copies.append(pltpu.make_async_copy(target_ref.at[r], place_ref.at[r], local.at[1]))
+    for copy in copies:
+        copy.start()
+    for copy in copies:
+        copy.wait()
+
+
+def exchange(outgoing, targets):
+    dma = pltpu.SemaphoreType.DMA
+    padded = jnp.pad(targets.reshape(ROWS, 1, CAP), ((0, 0), (0, 7), (0, 128 - CAP)))
+    arrived, places = pl.pallas_call(
+        exchange_kernel,
+        out_shape=(
+            jax.ShapeDtypeStruct(outgoing.shape, outgoing.dtype),
+            jax.ShapeDtypeStruct(padded.shape, padded.dtype),
+        ),
+        in_specs=[ANY, ANY],
+        out_specs=(ANY, ANY),
+        scratch_shapes=[dma((15,)), dma((15,)), dma((15,)), dma((15,)), dma((2,))],
+        compiler_params=pltpu.CompilerParams(has_side_effects=True),
+        name="exchange",
+    )(outgoing, padded)
+    return arrived, places[:, 0, :CAP].reshape(SLOTS)
 
 
 def build_lists(places_ref, head_ref, next_ref):
@@ -201,17 +254,22 @@
     )(places, front_init, arrived)
 
 
+PARTS = 8
+SUB = 128 // PARTS
+CHIPS = ((2, 1), (1, 1), (3, 1), (2, 0), (0, 1), (1, 0), (3, 0))
+
+
 def spread_kernel(
     p_ref, prs_ref, wa_ref, a_ref, w_ref, stage_ref,
-    s_pr1, r_pr1, s_swap, r_swap, s_pr2, r_pr2, s_pr3, r_pr3, s_ps2, r_ps2, s_ps3, r_ps3,
+    s_pr1, r_pr1, s_swap, r_swap, s_pry, r_pry, s_pr3, r_pr3, s_ps2, r_ps2, s_ps3, r_ps3,
     s_w1, r_w1, s_w2, r_w2, s_w3, r_w3, s_w4, r_w4, local,
 ):
     r = lax.axis_index("row")
     c = lax.axis_index("col")
     m, k = r // 2, r % 2
+    x, y = m // 2, m % 2
     yh, z = c // 4, c % 4
     root = (r == 0) & (c == 0)
-    pair = (r, lax.rem(c + 4, 8))
     other_core = (2 * m + 1 - k, c)
 
     def remote(src, dst, send, recv, dev):
@@ -227,37 +285,51 @@
 
         lax.fori_loop(lo, hi, step, 0)
 
-    mine = rows(128 * c, 128)
-    theirs = rows(128 * lax.rem(c + 4, 8), 128)
-
-    def pr1(i):
-        part = rows(128 * i, 128)
-        return remote(p_ref.at[part], prs_ref.at[part], s_pr1.at[i], r_pr1.at[0], (r, i))
-
-    def pr2():
-        return remote(prs_ref.at[mine], prs_ref.at[mine], s_pr2.at[0], r_pr2.at[0], pair)
-
-    def pr3(dz, which):
-        part = (mine, theirs)[which]
-        i = (dz - 1) * 2 + which
+    to_m = [m] + [lax.rem(x + dx, 4) * 2 + lax.rem(y + dy, 2) for dx, dy in CHIPS]
+    from_m = [m] + [lax.rem(x + 4 - dx, 4) * 2 + lax.rem(y + dy, 2) for dx, dy in CHIPS]
+
+    def piece_at(position):
+        px, py = position // 2, position % 2
+        turn = lax.rem(px + 4 - c // 2, 4)
+        return (turn // 2) * 4 + lax.rem(turn, 2) * 2 + lax.rem(py + 2 - c % 2, 2)
+
+    def part_of(piece, ch):
+        return rows(128 * piece + SUB * ch, SUB)
+
+    def pr1(ch, i, half):
+        part = part_of(i + 4 * half, ch)
+        j = (ch * 4 + i) * 2 + half
+        return remote(p_ref.at[part], prs_ref.at[part], s_pr1.at[j], r_pr1.at[ch * 2 + half], (r, i))
+
+    def pry(ch, half):
+        part = part_of(z + 4 * half, ch)
+        j = ch * 2 + half
+        return remote(prs_ref.at[part], prs_ref.at[part], s_pry.at[j], r_pry.at[j], (r, z + 4))
+
+    def pr3(ch, dz, half):
+        part = part_of(z + 4 * half, ch)
+        i = ch * 6 + (dz - 1) * 2 + half
         return remote(
             prs_ref.at[part], prs_ref.at[part], s_pr3.at[i], r_pr3.at[i], (r, yh * 4 + lax.rem(z + dz, 4))
         )
 
-    def swap():
-        there = rows(PW + PW * k + 128 * c, 128)
-        return remote(prs_ref.at[mine], prs_ref.at[there], s_swap.at[0], r_swap.at[0], (2 * c + k, m))
-
-    def ps_rows(o):
-        return rows(PW + PW * k + 128 * lax.rem(m + 8 - o, 8), 128)
-
-    def ps2(o):
-        part = ps_rows(0)
-        return remote(prs_ref.at[part], prs_ref.at[part], s_ps2.at[o], r_ps2.at[o], (2 * lax.rem(m + o, 8) + k, c))
-
-    def ps3(o):
-        part = ps_rows(o)
-        return remote(prs_ref.at[part], prs_ref.at[part], s_ps3.at[o], r_ps3.at[o], other_core)
+    def swap(ch):
+        there = rows(PW + PW * k + 128 * c + SUB * ch, SUB)
+        spot = lax.rem(yh * 2 + z // 2 + x, 4) * 2 + lax.rem(z + y, 2)
+        return remote(prs_ref.at[part_of(c, ch)], prs_ref.at[there], s_swap.at[ch], r_swap.at[ch], (2 * spot + k, m))
+
+    def ps_rows(ch, o):
+        return rows(PW + PW * k + 128 * piece_at(from_m[o]) + SUB * ch, SUB)
+
+    def ps2(ch, o):
+        part = ps_rows(ch, 0)
+        i = ch * 8 + o
+        return remote(prs_ref.at[part], prs_ref.at[part], s_ps2.at[i], r_ps2.at[i], (2 * to_m[o] + k, c))
+
+    def ps3(ch, o):
+        part = ps_rows(ch, o)
+        i = ch * 8 + o
+        return remote(prs_ref.at[part], prs_ref.at[part], s_ps3.at[i], r_ps3.at[i], other_core)
 
     def w1(q):
         part = rows(8 * q, 8)
@@ -268,11 +340,11 @@
         return remote(wa_ref.at[part], wa_ref.at[part], s_w2.at[o], r_w2.at[o], (r, lax.rem(c + o, 8)))
 
     def w_rows(o):
-        return rows(64 * (2 * lax.rem(m + 8 - o, 8) + k), 64)
+        return rows(64 * (2 * from_m[o] + k), 64)
 
     def w3(o):
         part = w_rows(0)
-        return remote(wa_ref.at[part], wa_ref.at[part], s_w3.at[o], r_w3.at[o], (2 * lax.rem(m + o, 8) + k, c))
+        return remote(wa_ref.at[part], wa_ref.at[part], s_w3.at[o], r_w3.at[o], (2 * to_m[o] + k, c))
 
     def w4(o):
         part = w_rows(o)
@@ -283,49 +355,107 @@
         copy.start()
         copy.wait()
 
+    stays = (m == 0) & (c == 0)
+
+    def send_parts(ch):
+        for i in (2, 1, 3):
+            for half in (0, 1):
+                pr1(ch, i, half).start()
+
     @pl.when(c == 0)
     def _():
-        for i in (4, 2, 6, 1, 3, 5, 7):
-            pr1(i).start()
-        move(p_ref.at[pl.ds(0, 128)], stage_ref, local.at[0])
-        move(stage_ref, prs_ref.at[pl.ds(0, 128)], local.at[1])
-
-    @pl.when(c > 0)
-    def _():
-        pr1(0).wait_recv()
-
-    pr2().start()
-
-    @pl.when(m == c)
-    def _():
-        move(prs_ref.at[mine], stage_ref, local.at[0])
-        move(stage_ref, prs_ref.at[ps_rows(0)], local.at[1])
-
-    @pl.when(m != c)
-    def _():
-        swap().start()
-
-    for dz in (2, 1, 3):
-        pr3(dz, 0).start()
-
-    @pl.when(m != c)
-    def _():
-        swap().wait_recv()
-
-    each(1, 8, lambda o: ps2(o).start())
-    ps3(0).start()
+        send_parts(0)
+        loads = [
+            pltpu.make_async_copy(p_ref.at[pl.ds(512 * h, 128)], stage_ref.at[pl.ds(128 * h, 128)], local.at[h])
+            for h in (0, 1)
+        ]
+        for copy in loads:
+            copy.start()
+        for copy in loads:
+            copy.wait()
+        stores = [
+            pltpu.make_async_copy(stage_ref.at[pl.ds(128 * h, 128)], prs_ref.at[pl.ds(512 * h, 128)], local.at[h])
+            for h in (0, 1)
+        ]
+        for copy in stores:
+            copy.start()
+
+        @pl.when(m == 0)
+        def _():
+            move(stage_ref.at[pl.ds(0, 128)], prs_ref.at[rows(PW + PW * k, 128)], local.at[2])
+
+        for copy in stores:
+            copy.wait()
+
+    def take(ch):
+        @pl.when((c == 0) & (ch > 0))
+        def _():
+            send_parts(ch)
+
+        @pl.when((yh == 0) & (z > 0))
+        def _():
+            for half in (0, 1):
+                pr1(ch, 0, half).wait_recv()
+
+        @pl.when(yh == 0)
+        def _():
+            for half in (1, 0):
+                pry(ch, half).start()
+
+        @pl.when(yh == 1)
+        def _():
+            for half in (1, 0):
+                pry(ch, half).wait_recv()
+
+        @pl.when(jnp.logical_not(stays))
+        def _():
+            swap(ch).start()
+
+        for dz in (2, 1, 3):
+            for half in (0, 1):
+                pr3(ch, dz, half).start()
+
+    def fan(ch):
+        @pl.when(jnp.logical_not(stays))
+        def _():
+            swap(ch).wait_recv()
+
+        for o in range(1, 8):
+            ps2(ch, o).start()
+        ps3(ch, 0).start()
+
+    def pipeline(i):
+        @pl.when(i < PARTS)
+        def _():
+            take(i)
+
+        @pl.when(i > 0)
+        def _():
+            fan(i - 1)
+
+    each(0, PARTS + 1, pipeline)
+
+    def send_block(step):
+        def send(i):
+            q = step * 16 + i
+
+            @pl.when(q > 0)
+            def _():
+                w1(q).start()
+
+        each(0, 16, send)
 
     @pl.when(root)
     def _():
         move(p_ref, w_ref, local.at[2])
         symmetrise(w_ref, a_ref)
-        chol_inverse(a_ref, w_ref)
-        each(1, ROWS * COLS, lambda q: w1(q).start())
+        chol_inverse(a_ref, w_ref, send_block)
         move(w_ref.at[pl.ds(0, 8)], wa_ref.at[pl.ds(0, 8)], local.at[2])
 
-    pr2().wait_recv()
-    for dz in (2, 1, 3):
-        pr3(dz, 1).start()
+    def cross(ch):
+        for o in range(1, 8):
+            ps2(ch, o).wait_recv()
+            ps3(ch, o).start()
 
     @pl.when(jnp.logical_not(root))
     def _():
@@ -333,55 +463,54 @@
 
     each(1, 8, lambda o: w2(o).start())
     each(1, 8, lambda o: w2(o).wait_recv())
-    each(1, 8, lambda o: w3(o).start())
+    for o in range(1, 8):
+        w3(o).start()
     w4(0).start()
-
-    def forward_ps(o):
-        ps2(o).wait_recv()
-        ps3(o).start()
-
-    each(1, 8, forward_ps)
-
-    def forward_w(o):
+    each(0, PARTS, cross)
+    for o in range(1, 8):
         w3(o).wait_recv()
         w4(o).start()
 
-    each(1, 8, forward_w)
-
     @pl.when(root)
     def _():
         each(1, ROWS * COLS, lambda q: w1(q).wait_send())
 
-    @pl.when(c == 0)
-    def _():
-        each(1, 8, lambda i: pr1(i).wait_send())
-
-    @pl.when(m != c)
-    def _():
-        swap().wait_send()
-
-    pr2().wait_send()
-    for dz in (1, 2, 3):
-        for which in (0, 1):
-            pr3(dz, which).wait()
-
-    def finish(o):
+    def finish(ch):
+        @pl.when(c == 0)
+        def _():
+            for i in (1, 2, 3):
+                for half in (0, 1):
+                    pr1(ch, i, half).wait_send()
+
+        @pl.when(yh == 0)
+        def _():
+            for half in (0, 1):
+                pry(ch, half).wait_send()
+
+        @pl.when(jnp.logical_not(stays))
+        def _():
+            swap(ch).wait_send()
+
+        for dz in (1, 2, 3):
+            for half in (0, 1):
+                pr3(ch, dz, half).wait()
+        for o in range(1, 8):
+            ps2(ch, o).wait_send()
+        for o in range(8):
+            ps3(ch, o).wait()
+
+    each(0, PARTS, finish)
+    for o in range(1, 8):
         w2(o).wait_send()
         w3(o).wait_send()
-        ps2(o).wait_send()
-
-    each(1, 8, finish)
-
-    def finish_core(o):
-        ps3(o).wait()
+    for o in range(8):
         w4(o).wait()
-
-    each(0, 8, finish_core)
 
 
 def spread(panel):
     dma = pltpu.SemaphoreType.DMA
-    sizes = [8, 1, 1, 1, 1, 1, 6, 6, 8, 8, 8, 8, 128, 1, 8, 8, 8, 8, 8, 8, 3]
+    n = PARTS
+    sizes = [8 * n, 2 * n, n, n, 2 * n, 2 * n, 6 * n, 6 * n, 8 * n, 8 * n, 8 * n, 8 * n, 128, 1, 8, 8, 8, 8, 8, 8, 3]
     return pl.pallas_call(
         spread_kernel,
         out_shape=(
@@ -393,7 +522,7 @@
         scratch_shapes=[
             pltpu.VMEM((PW, PW), jnp.float32),
             pltpu.VMEM((PW, PW), jnp.float32),
-            pltpu.VMEM((128, PW), jnp.float32),
+            pltpu.VMEM((256, PW), jnp.float32),
         ]
         + [dma((size,)) for size in sizes],
         compiler_params=pltpu.CompilerParams(has_side_effects=True, vmem_limit_bytes=40 * MIB),
@@ -489,8 +618,7 @@
 
 def body(front_init, child_tiles, child_dest):
     outgoing, targets = pack(child_tiles, child_dest)
-    arrived = lax.all_to_all(outgoing, "row", split_axis=0, concat_axis=0, tiled=True)
-    places = lax.all_to_all(targets, "row", split_axis=0, concat_axis=0, tiled=True)
+    arrived, places = exchange(outgoing, targets)
     panel = panel_sum(places, front_init, arrived)
     strips, inverse = spread(panel)
     return update(places, inverse, strips, front_init, arrived)

time: 461 us -> 366 us (0.79)
  the two profiles are of different devices: /device:TPU:45 before, /device:TPU:5 now
where the time goes in v3:
time: 366 us; the launch traced here: 360 us
  Pallas kernels  343 us (94%)
  local copies, waits for them, and re-layouts  16.6 us (5%)
    pallas_call x1, Pallas kernels, spread(): pl.pallas_call(spread_kernel, out_shape=(jax.ShapeDtypeStruct((3 * PW, PW...  172 us
    pallas_call x1, Pallas kernels, exchange(): pl.pallas_call(exchange_kernel, out_shape=(jax.ShapeDtypeStruct(outgoing....  106 us
    pallas_call x1, Pallas kernels, update(): pl.pallas_call(update_kernel, grid=(FILL + 8,), out_shape=(jax.ShapeDtype...  53.5 us
    unnamed x14, local copies, waits for them, and re-layouts  15 us
    pallas_call x1, Pallas kernels, pack(): pl.pallas_call(pack_kernel, out_shape=(jax.ShapeDtypeStruct((SLOTS, TW, T...  7.98 us

profile of v3, /device:TPU:5, one launch (start us, length us, event | category | flops | bytes accessed | tf_op | source)
XLA Modules:
  0.0 360.4 jit_solution(80633799886229069)
XLA Ops:
  0.6 0.0 copy-start.4
  0.6 2.2 copy-done.4
  2.8 0.0 copy-start.6
  2.8 0.7 copy-done.6
  3.5 8.0 %pack.1 = (bf16[64,256,256]{2,1,0:T(8,128)(2,1)S(1)}, s32[64]{0:T(128)S(1)}) custom-call(s32[32]{0:T(128)S(1)} %copy-done.6, bf16[32,256,256]{2,1,0:T(8,128)(2,1)S(1)} %copy-done.4), custom_call_target="tpu_custom_call" | custom-call | tf_op jit(solution)/shard_map/pack/pallas_call | solution.py:131
  11.5 0.0 copy-start.2
  11.5 3.4 copy-done.2
  14.9 0.1 reshape.7
  14.9 0.6 pad.4.target_ref
  15.6 105.7 %exchange.1 = (bf16[64,256,256]{2,1,0:T(8,128)(2,1)}, s32[16,8,128]{2,1,0:T(8,128)}) custom-call(bf16[64,256,256]{2,1,0:T(8,128)(2,1)} %copy-done.2, s32[16,8,128]{2,1,0:T(8,128)} %pad.4.target_ref), custom_call_target="tpu_custom_call" | custom-call | tf_op jit(solution)/shard_map/exchange/pallas_call | solution.py:182
  121.3 0.9 slice_reduce_fusion
  122.2 0.1 reshape_squeeze.3.places_ref
  122.3 0.0 copy-start
  122.3 3.4 copy-done
  125.7 0.0 copy-start.1
  125.7 3.4 copy-done.1
  129.0 0.0 copy-start.5
  129.0 3.3 panel_sum.1.p_ref
  132.4 0.0 copy-done.5
  132.4 172.5 %spread.1 = (f32[3072,1024]{1,0:T(8,128)}, f32[1024,1024]{1,0:T(8,128)S(1)}) custom-call(f32[1024,1024]{1,0:T(8,128)S(1)} %panel_sum.1.p_ref), custom_call_target="tpu_custom_call" | custom-call | tf_op jit(solution)/shard_map/spread/pallas_call | solution.py:514
  304.9 0.0 copy-start.3
  304.9 2.0 copy-done.3
  306.9 53.5 %update.1 = (f32[1024,1024]{1,0:T(8,128)}, f32[1024,2048]{1,0:T(8,128)}) custom-call(s32[64]{0:T(128)} %copy-done.5, f32[1024,1024]{1,0:T(8,128)} %copy-done.3, f32[3072,1024]{1,0:T(8,128)} %get-tuple-element.13.prs_ref, f32[1024,2048]{1,0:T(8,128)} %front_ref.3, bf16[64,256,256]{2,1,0:T(8,128)(2,1)} %get-tuple-element.11.arrived_ref), custom_call_target="tpu_custom_call" | custom-call | tf_op jit(solution)/shard_map/update/pallas_call | solution.py:588
Async XLA Ops:
  0.6 2.2 copy-start.4
  2.8 0.7 copy-start.6
  11.5 3.4 copy-start.2
  122.3 3.4 copy-start
  125.7 3.4 copy-start.1
  129.0 3.3 copy-start.5
  304.9 2.0 copy-start.3

commit v4 on v3

--- a/solution.py
+++ b/solution.py
@@ -137,7 +137,7 @@
         in_specs=[pl.BlockSpec(memory_space=pltpu.SMEM), pl.BlockSpec(memory_space=pltpu.VMEM)],
         out_specs=(ANY, pl.BlockSpec(memory_space=pltpu.SMEM)),
         scratch_shapes=[pltpu.SMEM((ROWS,), jnp.int32), pltpu.SemaphoreType.DMA((count,))],
-        compiler_params=pltpu.CompilerParams(vmem_limit_bytes=16 * MIB),
+        compiler_params=pltpu.CompilerParams(vmem_limit_bytes=58 * MIB),
         name="pack",
     )(child_dest, child_tiles)
 
@@ -249,19 +249,22 @@
         ],
         out_specs=pl.BlockSpec((TW, TW), lambda i: (i // 4, i % 4)),
         scratch_shapes=[pltpu.SMEM((32,), jnp.int32), pltpu.SMEM((SLOTS,), jnp.int32)],
-        compiler_params=pltpu.CompilerParams(vmem_limit_bytes=24 * MIB),
+        compiler_params=pltpu.CompilerParams(vmem_limit_bytes=58 * MIB),
         name="panel_sum",
     )(places, front_init, arrived)
 
 
 PARTS = 8
+LAG = 1
 SUB = 128 // PARTS
+UPWARD = (1, 5, 2, 0)
+DOWNWARD = (3, 7, 6, 4)
 CHIPS = ((2, 1), (1, 1), (3, 1), (2, 0), (0, 1), (1, 0), (3, 0))
 
 
 def spread_kernel(
-    p_ref, prs_ref, wa_ref, a_ref, w_ref, stage_ref,
-    s_pr1, r_pr1, s_swap, r_swap, s_pry, r_pry, s_pr3, r_pr3, s_ps2, r_ps2, s_ps3, r_ps3,
+    p_ref, prs_ref, wa_ref, a_ref, w_ref,
+    s_flow, r_flow, s_swap, r_swap, s_pry, r_pry, s_pr3, r_pr3, s_ps2, r_ps2, s_ps3, r_ps3,
     s_w1, r_w1, s_w2, r_w2, s_w3, r_w3, s_w4, r_w4, local,
 ):
     r = lax.axis_index("row")
@@ -296,10 +299,11 @@
     def part_of(piece, ch):
         return rows(128 * piece + SUB * ch, SUB)
 
-    def pr1(ch, i, half):
-        part = part_of(i + 4 * half, ch)
-        j = (ch * 4 + i) * 2 + half
-        return remote(p_ref.at[part], prs_ref.at[part], s_pr1.at[j], r_pr1.at[ch * 2 + half], (r, i))
+    def flow(ch, piece, src):
+        part = part_of(piece, ch)
+        there = lax.rem(z + (1 if piece in UPWARD else 3), 4)
+        i = ch * 8 + piece
+        return remote(src.at[part], prs_ref.at[part], s_flow.at[i], r_flow.at[i], (r, there))
 
     def pry(ch, half):
         part = part_of(z + 4 * half, ch)
@@ -358,44 +362,40 @@
     stays = (m == 0) & (c == 0)
 
     def send_parts(ch):
-        for i in (2, 1, 3):
-            for half in (0, 1):
-                pr1(ch, i, half).start()
+        for up, down in zip(UPWARD, DOWNWARD):
+            flow(ch, up, p_ref).start()
+            flow(ch, down, p_ref).start()
 
     @pl.when(c == 0)
     def _():
         send_parts(0)
-        loads = [
-            pltpu.make_async_copy(p_ref.at[pl.ds(512 * h, 128)], stage_ref.at[pl.ds(128 * h, 128)], local.at[h])
-            for h in (0, 1)
-        ]
-        for copy in loads:
-            copy.start()
-        for copy in loads:
-            copy.wait()
-        stores = [
-            pltpu.make_async_copy(stage_ref.at[pl.ds(128 * h, 128)], prs_ref.at[pl.ds(512 * h, 128)], local.at[h])
-            for h in (0, 1)
-        ]
-        for copy in stores:
-            copy.start()
+        move(p_ref, w_ref, local.at[0])
+        move(w_ref, prs_ref.at[pl.ds(0, PW)], local.at[1])
 
         @pl.when(m == 0)
         def _():
-            move(stage_ref.at[pl.ds(0, 128)], prs_ref.at[rows(PW + PW * k, 128)], local.at[2])
-
-        for copy in stores:
-            copy.wait()
+            move(w_ref.at[pl.ds(0, 128)], prs_ref.at[rows(PW + PW * k, 128)], local.at[2])
+
+    rises = (yh == 0) & ((z == 1) | (z == 2))
+    falls = (yh == 0) & ((z == 2) | (z == 3))
+
+    def forward(ch, pieces):
+        for piece in pieces:
+            flow(ch, piece, prs_ref).wait_recv()
+            flow(ch, piece, prs_ref).start()
 
     def take(ch):
         @pl.when((c == 0) & (ch > 0))
         def _():
             send_parts(ch)
 
-        @pl.when((yh == 0) & (z > 0))
-        def _():
-            for half in (0, 1):
-                pr1(ch, 0, half).wait_recv()
+        @pl.when(rises)
+        def _():
+            forward(ch, UPWARD)
+
+        @pl.when(falls)
+        def _():
+            forward(ch, DOWNWARD)
 
         @pl.when(yh == 0)
         def _():
@@ -411,9 +411,11 @@
         def _():
             swap(ch).start()
 
-        for dz in (2, 1, 3):
-            for half in (0, 1):
-                pr3(ch, dz, half).start()
+        @pl.when(yh == 1)
+        def _():
+            for dz in (2, 1, 3):
+                for half in (0, 1):
+                    pr3(ch, dz, half).start()
 
     def fan(ch):
         @pl.when(jnp.logical_not(stays))
@@ -429,11 +431,11 @@
         def _():
             take(i)
 
-        @pl.when(i > 0)
-        def _():
-            fan(i - 1)
-
-    each(0, PARTS + 1, pipeline)
+        @pl.when(i >= LAG)
+        def _():
+            fan(i - LAG)
+
+    each(0, PARTS, pipeline)
 
     def send_block(step):
         def send(i):
@@ -447,15 +449,9 @@
 
     @pl.when(root)
     def _():
-        move(p_ref, w_ref, local.at[2])
         symmetrise(w_ref, a_ref)
         chol_inverse(a_ref, w_ref, send_block)
         move(w_ref.at[pl.ds(0, 8)], wa_ref.at[pl.ds(0, 8)], local.at[2])
-
-    def cross(ch):
-        for o in range(1, 8):
-            ps2(ch, o).wait_recv()
-            ps3(ch, o).start()
 
     @pl.when(jnp.logical_not(root))
     def _():
@@ -466,6 +462,13 @@
     for o in range(1, 8):
         w3(o).start()
     w4(0).start()
+    each(PARTS, PARTS + LAG, pipeline)
+
+    def cross(ch):
+        for o in range(1, 8):
+            ps2(ch, o).wait_recv()
+            ps3(ch, o).start()
+
     each(0, PARTS, cross)
     for o in range(1, 8):
         w3(o).wait_recv()
@@ -476,11 +479,26 @@
         each(1, ROWS * COLS, lambda q: w1(q).wait_send())
 
     def finish(ch):
-        @pl.when(c == 0)
-        def _():
-            for i in (1, 2, 3):
-                for half in (0, 1):
-                    pr1(ch, i, half).wait_send()
+        def settle(pieces, done):
+            for piece in pieces:
+                copy = flow(ch, piece, prs_ref)
+                copy.wait_send() if done else copy.wait_recv()
+
+        @pl.when(rises | (c == 0))
+        def _():
+            settle(UPWARD, True)
+
+        @pl.when(falls | (c == 0))
+        def _():
+            settle(DOWNWARD, True)
+
+        @pl.when((yh == 0) & (z == 1))
+        def _():
+            settle(DOWNWARD, False)
+
+        @pl.when((yh == 0) & (z == 3))
+        def _():
+            settle(UPWARD, False)
 
         @pl.when(yh == 0)
         def _():
@@ -491,9 +509,12 @@
         def _():
             swap(ch).wait_send()
 
-        for dz in (1, 2, 3):
-            for half in (0, 1):
-                pr3(ch, dz, half).wait()
+        @pl.when(yh == 1)
+        def _():
+            for dz in (1, 2, 3):
+                for half in (0, 1):
+                    pr3(ch, dz, half).wait()
+
         for o in range(1, 8):
             ps2(ch, o).wait_send()
         for o in range(8):
@@ -510,7 +531,7 @@
 def spread(panel):
     dma = pltpu.SemaphoreType.DMA
     n = PARTS
-    sizes = [8 * n, 2 * n, n, n, 2 * n, 2 * n, 6 * n, 6 * n, 8 * n, 8 * n, 8 * n, 8 * n, 128, 1, 8, 8, 8, 8, 8, 8, 3]
+    sizes = [8 * n, 8 * n, n, n, 2 * n, 2 * n, 6 * n, 6 * n, 8 * n, 8 * n, 8 * n, 8 * n, 128, 1, 8, 8, 8, 8, 8, 8, 3]
     return pl.pallas_call(
         spread_kernel,
         out_shape=(
@@ -522,10 +543,9 @@
         scratch_shapes=[
             pltpu.VMEM((PW, PW), jnp.float32),
             pltpu.VMEM((PW, PW), jnp.float32),
-            pltpu.VMEM((256, PW), jnp.float32),
         ]
         + [dma((size,)) for size in sizes],
-        compiler_params=pltpu.CompilerParams(has_side_effects=True, vmem_limit_bytes=40 * MIB),
+        compiler_params=pltpu.CompilerParams(has_side_effects=True, vmem_limit_bytes=58 * MIB),
         name="spread",
     )(panel)
 

time: 366 us -> 335 us (0.915); the launches traced: 360 us -> 334 us
  local copies, waits for them, and re-layouts: 16.6 us -> 2.84 us
  Pallas kernels: 343 us -> 330 us
    pallas_call x1, Pallas kernels: 172 us -> 152 us  [spread(): pl.pallas_call(spread_kernel, out_shape=(jax.ShapeDtypeStruct((3 * PW, PW...]
    unnamed x14 -> x0, local copies, waits for them, and re-layouts: 15 us -> none
    pallas_call x1, Pallas kernels: 3.31 us -> 13.8 us  [panel_sum(): pl.pallas_call(panel_kernel, grid=(16,), out_shape=jax.ShapeDtypeStruct((...]
where the time goes in v4:
time: 335 us; the launch traced here: 334 us
  Pallas kernels  330 us (99%)
    pallas_call x1, Pallas kernels, spread(): pl.pallas_call(spread_kernel, out_shape=(jax.ShapeDtypeStruct((3 * PW, PW...  152 us
    pallas_call x1, Pallas kernels, exchange(): pl.pallas_call(exchange_kernel, out_shape=(jax.ShapeDtypeStruct(outgoing....  106 us
    pallas_call x1, Pallas kernels, update(): pl.pallas_call(update_kernel, grid=(FILL + 8,), out_shape=(jax.ShapeDtype...  53.5 us
    pallas_call x1, Pallas kernels, panel_sum(): pl.pallas_call(panel_kernel, grid=(16,), out_shape=jax.ShapeDtypeStruct((...  13.8 us

profile of v4, /device:TPU:5, one launch (start us, length us, event | category | flops | bytes accessed | tf_op | source)
XLA Modules:
  0.0 333.6 jit_solution(8795919246966352174)
XLA Ops:
  0.6 5.5 %pack.1 = (bf16[64,256,256]{2,1,0:T(8,128)(2,1)}, s32[64]{0:T(128)}) custom-call(s32[32]{0:T(128)} %dest_ref.1, bf16[32,256,256]{2,1,0:T(8,128)(2,1)} %tiles_ref.1), custom_call_target="tpu_custom_call" | custom-call | tf_op jit(solution)/shard_map/pack/pallas_call | solution.py:131
  6.1 0.7 reshape.7
  6.9 0.6 pad.4.target_ref
  7.5 105.7 %exchange.1 = (bf16[64,256,256]{2,1,0:T(8,128)(2,1)}, s32[16,8,128]{2,1,0:T(8,128)}) custom-call(bf16[64,256,256]{2,1,0:T(8,128)(2,1)} %get-tuple-element.8.out_ref, s32[16,8,128]{2,1,0:T(8,128)} %pad.4.target_ref), custom_call_target="tpu_custom_call" | custom-call | tf_op jit(solution)/shard_map/exchange/pallas_call | solution.py:182
  113.2 0.9 slice_reduce_fusion
  114.1 0.6 reshape_squeeze.3.places_ref
  114.7 13.8 %panel_sum.1.p_ref = f32[1024,1024]{1,0:T(8,128)} custom-call(s32[64]{0:T(128)} %reshape_squeeze.3.places_ref, f32[1024,2048]{1,0:T(8,128)} %front_ref.3, bf16[64,256,256]{2,1,0:T(8,128)(2,1)} %get-tuple-element.11.arrived_ref), custom_call_target="tpu_custom_call" | custom-call | tf_op jit(solution)/shard_map/panel_sum/pallas_call | solution.py:241
  128.5 151.6 %spread.1 = (f32[3072,1024]{1,0:T(8,128)}, f32[1024,1024]{1,0:T(8,128)}) custom-call(f32[1024,1024]{1,0:T(8,128)} %panel_sum.1.p_ref), custom_call_target="tpu_custom_call" | custom-call | tf_op jit(solution)/shard_map/spread/pallas_call | solution.py:535
  280.1 53.5 %update.1 = (f32[1024,1024]{1,0:T(8,128)}, f32[1024,2048]{1,0:T(8,128)}) custom-call(s32[64]{0:T(128)} %reshape_squeeze.3.places_ref, f32[1024,1024]{1,0:T(8,128)} %get-tuple-element.12.w_ref, f32[3072,1024]{1,0:T(8,128)} %get-tuple-element.13.prs_ref, f32[1024,2048]{1,0:T(8,128)} %front_ref.3, bf16[64,256,256]{2,1,0:T(8,128)(2,1)} %get-tuple-element.11.arrived_ref), custom_call_target="tpu_custom_call" | custom-call | tf_op jit(solution)/shard_map/update/pallas_call | solution.py:608

commit v5 on v4

--- a/solution.py
+++ b/solution.py
@@ -215,40 +215,66 @@
     lax.fori_loop(0, SLOTS, link, 0)
 
 
-def add_children(tile, total_ref, arrived_ref, head_ref, next_ref):
+def walk(tile, head_ref, next_ref, visit):
     def more(slot):
         return slot >= 0
 
+    def step(slot):
+        visit(slot)
+        return next_ref[slot]
+
+    lax.while_loop(more, step, head_ref[tile])
+
+
+def fetch(arrived_ref, tiles_ref, sems, slot):
+    return pltpu.make_async_copy(arrived_ref.at[slot], tiles_ref.at[slot], sems.at[slot])
+
+
+def fetch_tiles(tiles, arrived_ref, tiles_ref, sems, head_ref, next_ref):
+    for tile in tiles:
+        walk(tile, head_ref, next_ref, lambda slot: fetch(arrived_ref, tiles_ref, sems, slot).start())
+
+
+def add_children(tile, total_ref, arrived_ref, tiles_ref, sems, head_ref, next_ref):
     def add(slot):
-        total_ref[...] += arrived_ref[slot].astype(jnp.float32)
-        return next_ref[slot]
-
-    lax.while_loop(more, add, head_ref[tile])
-
-
-def panel_kernel(places_ref, front_ref, arrived_ref, out_ref, head_ref, next_ref):
+        fetch(arrived_ref, tiles_ref, sems, slot).wait()
+        total_ref[...] += tiles_ref[slot].astype(jnp.float32)
+
+    walk(tile, head_ref, next_ref, add)
+
+
+def panel_kernel(places_ref, front_ref, arrived_ref, out_ref, tiles_ref, sems, head_ref, next_ref):
     step = pl.program_id(0)
 
     @pl.when(step == 0)
     def _():
         build_lists(places_ref, head_ref, next_ref)
+        tiles = [8 * i + j for i in range(4) for j in range(PW // TW)]
+        fetch_tiles(tiles, arrived_ref, tiles_ref, sems, head_ref, next_ref)
 
     out_ref[...] = front_ref[...]
-    add_children((step // 4) * 8 + step % 4, out_ref, arrived_ref, head_ref, next_ref)
+    for j in range(PW // TW):
+        total = out_ref.at[:, j * TW : (j + 1) * TW]
+        add_children(step * 8 + j, total, arrived_ref, tiles_ref, sems, head_ref, next_ref)
 
 
 def panel_sum(places, front_init, arrived):
     return pl.pallas_call(
         panel_kernel,
-        grid=(16,),
+        grid=(front_init.shape[0] // TW,),
         out_shape=jax.ShapeDtypeStruct((front_init.shape[0], PW), jnp.float32),
         in_specs=[
             pl.BlockSpec(memory_space=pltpu.SMEM),
-            pl.BlockSpec((TW, TW), lambda i: (i // 4, i % 4)),
-            pl.BlockSpec((SLOTS, TW, TW), lambda i: (0, 0, 0), pipeline_mode=pl.Buffered(1)),
+            pl.BlockSpec((TW, PW), lambda i: (i, 0)),
+            ANY,
         ],
-        out_specs=pl.BlockSpec((TW, TW), lambda i: (i // 4, i % 4)),
-        scratch_shapes=[pltpu.SMEM((32,), jnp.int32), pltpu.SMEM((SLOTS,), jnp.int32)],
+        out_specs=pl.BlockSpec((TW, PW), lambda i: (i, 0)),
+        scratch_shapes=[
+            pltpu.VMEM((SLOTS, TW, TW), jnp.bfloat16),
+            pltpu.SemaphoreType.DMA((SLOTS,)),
+            pltpu.SMEM((32,), jnp.int32),
+            pltpu.SMEM((SLOTS,), jnp.int32),
+        ],
         compiler_params=pltpu.CompilerParams(vmem_limit_bytes=58 * MIB),
         name="panel_sum",
     )(places, front_init, arrived)
@@ -346,13 +372,17 @@
     def w_rows(o):
         return rows(64 * (2 * from_m[o] + k), 64)
 
-    def w3(o):
-        part = w_rows(0)
-        return remote(wa_ref.at[part], wa_ref.at[part], s_w3.at[o], r_w3.at[o], (2 * to_m[o] + k, c))
-
-    def w4(o):
-        part = w_rows(o)
-        return remote(wa_ref.at[part], wa_ref.at[part], s_w4.at[o], r_w4.at[o], other_core)
+    halves = (pl.ds(0, PW // 2), pl.ds(PW // 2, PW // 2))
+
+    def w3(o, half):
+        part = wa_ref.at[w_rows(0), halves[half]]
+        i = half * 8 + o
+        return remote(part, part, s_w3.at[i], r_w3.at[i], (2 * to_m[o] + k, c))
+
+    def w4(o, half):
+        part = wa_ref.at[w_rows(o), halves[half]]
+        i = half * 8 + o
+        return remote(part, part, s_w4.at[i], r_w4.at[i], other_core)
 
     def move(src, dst, sem):
         copy = pltpu.make_async_copy(src, dst, sem)
@@ -460,8 +490,15 @@
     each(1, 8, lambda o: w2(o).start())
     each(1, 8, lambda o: w2(o).wait_recv())
     for o in range(1, 8):
-        w3(o).start()
-    w4(0).start()
+        w3(o, 0).start()
+    w4(0, 0).start()
+
+    @pl.when(m >= 4)
+    def _():
+        for o in range(1, 8):
+            w3(o, 1).start()
+        w4(0, 1).start()
+
     each(PARTS, PARTS + LAG, pipeline)
 
     def cross(ch):
@@ -471,8 +508,14 @@
 
     each(0, PARTS, cross)
     for o in range(1, 8):
-        w3(o).wait_recv()
-        w4(o).start()
+        w3(o, 0).wait_recv()
+        w4(o, 0).start()
+
+        @pl.when(from_m[o] >= 4)
+        def _(o=o):
+            w3(o, 1).wait_recv()
+            w4(o, 1).start()
+
 
     @pl.when(root)
     def _():
@@ -523,15 +566,24 @@
     each(0, PARTS, finish)
     for o in range(1, 8):
         w2(o).wait_send()
-        w3(o).wait_send()
+        w3(o, 0).wait_send()
     for o in range(8):
-        w4(o).wait()
+        w4(o, 0).wait()
+
+        @pl.when(from_m[o] >= 4)
+        def _(o=o):
+            w4(o, 1).wait()
+
+    @pl.when(m >= 4)
+    def _():
+        for o in range(1, 8):
+            w3(o, 1).wait_send()
 
 
 def spread(panel):
     dma = pltpu.SemaphoreType.DMA
     n = PARTS
-    sizes = [8 * n, 8 * n, n, n, 2 * n, 2 * n, 6 * n, 6 * n, 8 * n, 8 * n, 8 * n, 8 * n, 128, 1, 8, 8, 8, 8, 8, 8, 3]
+    sizes = [8 * n, 8 * n, n, n, 2 * n, 2 * n, 6 * n, 6 * n, 8 * n, 8 * n, 8 * n, 8 * n, 128, 1, 8, 8, 16, 16, 16, 16, 3]
     return pl.pallas_call(
         spread_kernel,
         out_shape=(
@@ -563,27 +615,29 @@
 
 
 CHUNK = 512
+WIDE = 512
 FILL = 3 * PW // CHUNK
 
 
 def update_kernel(
     places_ref, w_ref, prs_ref, front_ref, arrived_ref, factor_ref, schur_ref,
-    wh_ref, wl_ref, fh_ref, fl_ref, head_ref, next_ref,
+    wh_ref, wl_ref, fh_ref, fl_ref, tiles_ref, sems, head_ref, next_ref,
 ):
     step = pl.program_id(0)
 
     @pl.when(step == 0)
     def _():
         build_lists(places_ref, head_ref, next_ref)
+        fetch_tiles(range(32), arrived_ref, tiles_ref, sems, head_ref, next_ref)
         wh_ref[...], wl_ref[...] = split(w_ref[...])
 
     @pl.when(step < FILL)
     def _():
         ah, al = split(prs_ref[...])
         here = pl.ds(pl.multiple_of(step * CHUNK, CHUNK), CHUNK)
-        for j in range(PW // TW):
-            out = slice(j * TW, (j + 1) * TW)
-            deep = slice(0, (j + 1) * TW)
+        for j in range(PW // WIDE):
+            out = slice(j * WIDE, (j + 1) * WIDE)
+            deep = slice(0, (j + 1) * WIDE)
             block = dot3(ah[:, deep], al[:, deep], wh_ref[out, deep], wl_ref[out, deep])
             fh_ref[here, out], fl_ref[here, out] = split(block)
 
@@ -598,7 +652,7 @@
         schur_ref[...] = front_ref[...] - dot3(fh_ref[:PW, :], fl_ref[:PW, :], fh_ref[right, :], fl_ref[right, :])
         for i in range(PW // TW):
             total = schur_ref.at[i * TW : (i + 1) * TW, :]
-            add_children(i * 8 + column, total, arrived_ref, head_ref, next_ref)
+            add_children(i * 8 + column, total, arrived_ref, tiles_ref, sems, head_ref, next_ref)
 
 
 def update(places, inverse, strips, front_init, arrived):
@@ -617,7 +671,7 @@
             pl.BlockSpec((PW, PW), lambda i: (0, 0), pipeline_mode=pl.Buffered(1)),
             pl.BlockSpec((CHUNK, PW), lambda i: (jnp.minimum(i, FILL - 1), 0)),
             pl.BlockSpec((PW, TW), column_map),
-            pl.BlockSpec((SLOTS, TW, TW), lambda i: (0, 0, 0), pipeline_mode=pl.Buffered(1)),
+            ANY,
         ],
         out_specs=(
             pl.BlockSpec((CHUNK, PW), lambda i: (jnp.minimum(i, PW // CHUNK - 1), 0)),
@@ -628,6 +682,8 @@
             pltpu.VMEM((PW, PW), jnp.bfloat16),
             pltpu.VMEM((3 * PW, PW), jnp.bfloat16),
             pltpu.VMEM((3 * PW, PW), jnp.bfloat16),
+            pltpu.VMEM((SLOTS, TW, TW), jnp.bfloat16),
+            pltpu.SemaphoreType.DMA((SLOTS,)),
             pltpu.SMEM((32,), jnp.int32),
             pltpu.SMEM((SLOTS,), jnp.int32),
         ],

time: 335 us -> 312 us (0.931)
  Pallas kernels: 330 us -> 304 us
    pallas_call x1, Pallas kernels: 53.5 us -> 42.4 us  [update(): pl.pallas_call(update_kernel, grid=(FILL + 8,), out_shape=(jax.ShapeDtype...]
    pallas_call x1, Pallas kernels: 152 us -> 143 us  [spread(): pl.pallas_call(spread_kernel, out_shape=(jax.ShapeDtypeStruct((3 * PW, PW...]
    pallas_call x1, Pallas kernels: 13.8 us -> 7.43 us  [panel_sum(): pl.pallas_call(panel_kernel, grid=(front_init.shape[0] // TW,), out_shape...]
where the time goes in v5:
time: 312 us; the launch traced here: 307 us
  Pallas kernels  304 us (97%)
    pallas_call x1, Pallas kernels, spread(): pl.pallas_call(spread_kernel, out_shape=(jax.ShapeDtypeStruct((3 * PW, PW...  143 us
    pallas_call x1, Pallas kernels, exchange(): pl.pallas_call(exchange_kernel, out_shape=(jax.ShapeDtypeStruct(outgoing....  106 us
    pallas_call x1, Pallas kernels, update(): pl.pallas_call(update_kernel, grid=(FILL + 8,), out_shape=(jax.ShapeDtype...  42.4 us
    pallas_call x1, Pallas kernels, panel_sum(): pl.pallas_call(panel_kernel, grid=(front_init.shape[0] // TW,), out_shape...  7.43 us

profile of v5, /device:TPU:5, one launch (start us, length us, event | category | flops | bytes accessed | tf_op | source)
XLA Modules:
  0.0 307.3 jit_solution(10156686088123588916)
XLA Ops:
  0.6 5.5 %pack.1 = (bf16[64,256,256]{2,1,0:T(8,128)(2,1)}, s32[64]{0:T(128)}) custom-call(s32[32]{0:T(128)} %dest_ref.1, bf16[32,256,256]{2,1,0:T(8,128)(2,1)} %tiles_ref.1), custom_call_target="tpu_custom_call" | custom-call | tf_op jit(solution)/shard_map/pack/pallas_call | solution.py:131
  6.1 0.7 reshape.7
  6.9 0.6 pad.4.target_ref
  7.5 105.7 %exchange.1 = (bf16[64,256,256]{2,1,0:T(8,128)(2,1)}, s32[16,8,128]{2,1,0:T(8,128)}) custom-call(bf16[64,256,256]{2,1,0:T(8,128)(2,1)} %get-tuple-element.8.out_ref, s32[16,8,128]{2,1,0:T(8,128)} %pad.4.target_ref), custom_call_target="tpu_custom_call" | custom-call | tf_op jit(solution)/shard_map/exchange/pallas_call | solution.py:182
  113.2 0.9 slice_reduce_fusion
  114.1 0.6 reshape_squeeze.3.places_ref
  114.7 7.4 %panel_sum.1.p_ref = f32[1024,1024]{1,0:T(8,128)} custom-call(s32[64]{0:T(128)} %reshape_squeeze.3.places_ref, f32[1024,2048]{1,0:T(8,128)} %front_ref.3, bf16[64,256,256]{2,1,0:T(8,128)(2,1)} %get-tuple-element.11.arrived_ref), custom_call_target="tpu_custom_call" | custom-call | tf_op jit(solution)/shard_map/panel_sum/pallas_call | solution.py:262
  122.1 142.6 %spread.1 = (f32[3072,1024]{1,0:T(8,128)}, f32[1024,1024]{1,0:T(8,128)}) custom-call(f32[1024,1024]{1,0:T(8,128)} %panel_sum.1.p_ref), custom_call_target="tpu_custom_call" | custom-call | tf_op jit(solution)/shard_map/spread/pallas_call | solution.py:587
  264.7 42.4 %update.1 = (f32[1024,1024]{1,0:T(8,128)}, f32[1024,2048]{1,0:T(8,128)}) custom-call(s32[64]{0:T(128)} %reshape_squeeze.3.places_ref, f32[1024,1024]{1,0:T(8,128)} %get-tuple-element.12.w_ref, f32[3072,1024]{1,0:T(8,128)} %get-tuple-element.13.prs_ref, f32[1024,2048]{1,0:T(8,128)} %front_ref.3, bf16[64,256,256]{2,1,0:T(8,128)(2,1)} %get-tuple-element.11.arrived_ref), custom_call_target="tpu_custom_call" | custom-call | tf_op jit(solution)/shard_map/update/pallas_call | solution.py:662

commit v6 on v5

--- a/solution.py
+++ b/solution.py
@@ -648,11 +648,13 @@
     @pl.when(step >= FILL)
     def _():
         column = step - FILL
-        right = pl.ds(pl.multiple_of(PW + column * TW, TW), TW)
+        right = pl.ds(pl.multiple_of(PW + column * WIDE, WIDE), WIDE)
         schur_ref[...] = front_ref[...] - dot3(fh_ref[:PW, :], fl_ref[:PW, :], fh_ref[right, :], fl_ref[right, :])
         for i in range(PW // TW):
-            total = schur_ref.at[i * TW : (i + 1) * TW, :]
-            add_children(i * 8 + column, total, arrived_ref, tiles_ref, sems, head_ref, next_ref)
+            for j in range(WIDE // TW):
+                total = schur_ref.at[i * TW : (i + 1) * TW, j * TW : (j + 1) * TW]
+                tile = i * 8 + column * (WIDE // TW) + j
+                add_children(tile, total, arrived_ref, tiles_ref, sems, head_ref, next_ref)
 
 
 def update(places, inverse, strips, front_init, arrived):
@@ -661,7 +663,7 @@
 
     return pl.pallas_call(
         update_kernel,
-        grid=(FILL + 8,),
+        grid=(FILL + front_init.shape[1] // WIDE,),
         out_shape=(
             jax.ShapeDtypeStruct((PW, PW), jnp.float32),
             jax.ShapeDtypeStruct(front_init.shape, jnp.float32),
@@ -670,12 +672,12 @@
             pl.BlockSpec(memory_space=pltpu.SMEM),
             pl.BlockSpec((PW, PW), lambda i: (0, 0), pipeline_mode=pl.Buffered(1)),
             pl.BlockSpec((CHUNK, PW), lambda i: (jnp.minimum(i, FILL - 1), 0)),
-            pl.BlockSpec((PW, TW), column_map),
+            pl.BlockSpec((PW, WIDE), column_map),
             ANY,
         ],
         out_specs=(
             pl.BlockSpec((CHUNK, PW), lambda i: (jnp.minimum(i, PW // CHUNK - 1), 0)),
-            pl.BlockSpec((PW, TW), column_map),
+            pl.BlockSpec((PW, WIDE), column_map),
         ),
         scratch_shapes=[
             pltpu.VMEM((PW, PW), jnp.bfloat16),

time: 312 us -> 312 us (level)
  no operation moved by 1% of the time
where the time goes in v6:
time: 312 us; the launch traced here: 307 us
  Pallas kernels  303 us (97%)
    pallas_call x1, Pallas kernels, spread(): pl.pallas_call(spread_kernel, out_shape=(jax.ShapeDtypeStruct((3 * PW, PW...  142 us
    pallas_call x1, Pallas kernels, exchange(): pl.pallas_call(exchange_kernel, out_shape=(jax.ShapeDtypeStruct(outgoing....  106 us
    pallas_call x1, Pallas kernels, update(): pl.pallas_call(update_kernel, grid=(FILL + front_init.shape[1] // WIDE,),...  42 us
    pallas_call x1, Pallas kernels, panel_sum(): pl.pallas_call(panel_kernel, grid=(front_init.shape[0] // TW,), out_shape...  7.62 us

profile of v6, /device:TPU:5, one launch (start us, length us, event | category | flops | bytes accessed | tf_op | source)
XLA Modules:
  0.0 306.6 jit_solution(17973511765624945469)
XLA Ops:
  0.6 5.5 %pack.1 = (bf16[64,256,256]{2,1,0:T(8,128)(2,1)}, s32[64]{0:T(128)}) custom-call(s32[32]{0:T(128)} %dest_ref.1, bf16[32,256,256]{2,1,0:T(8,128)(2,1)} %tiles_ref.1), custom_call_target="tpu_custom_call" | custom-call | tf_op jit(solution)/shard_map/pack/pallas_call | solution.py:131
  6.1 0.7 reshape.7
  6.9 0.6 pad.4.target_ref
  7.5 105.7 %exchange.1 = (bf16[64,256,256]{2,1,0:T(8,128)(2,1)}, s32[16,8,128]{2,1,0:T(8,128)}) custom-call(bf16[64,256,256]{2,1,0:T(8,128)(2,1)} %get-tuple-element.8.out_ref, s32[16,8,128]{2,1,0:T(8,128)} %pad.4.target_ref), custom_call_target="tpu_custom_call" | custom-call | tf_op jit(solution)/shard_map/exchange/pallas_call | solution.py:182
  113.2 0.9 slice_reduce_fusion
  114.1 0.6 reshape_squeeze.3.places_ref
  114.7 7.6 %panel_sum.1.p_ref = f32[1024,1024]{1,0:T(8,128)} custom-call(s32[64]{0:T(128)} %reshape_squeeze.3.places_ref, f32[1024,2048]{1,0:T(8,128)} %front_ref.3, bf16[64,256,256]{2,1,0:T(8,128)(2,1)} %get-tuple-element.11.arrived_ref), custom_call_target="tpu_custom_call" | custom-call | tf_op jit(solution)/shard_map/panel_sum/pallas_call | solution.py:262
  122.3 142.1 %spread.1 = (f32[3072,1024]{1,0:T(8,128)}, f32[1024,1024]{1,0:T(8,128)}) custom-call(f32[1024,1024]{1,0:T(8,128)} %panel_sum.1.p_ref), custom_call_target="tpu_custom_call" | custom-call | tf_op jit(solution)/shard_map/spread/pallas_call | solution.py:587
  264.4 42.0 %update.1 = (f32[1024,1024]{1,0:T(8,128)}, f32[1024,2048]{1,0:T(8,128)}) custom-call(s32[64]{0:T(128)} %reshape_squeeze.3.places_ref, f32[1024,1024]{1,0:T(8,128)} %get-tuple-element.12.w_ref, f32[3072,1024]{1,0:T(8,128)} %get-tuple-element.13.prs_ref, f32[1024,2048]{1,0:T(8,128)} %front_ref.3, bf16[64,256,256]{2,1,0:T(8,128)(2,1)} %get-tuple-element.11.arrived_ref), custom_call_target="tpu_custom_call" | custom-call | tf_op jit(solution)/shard_map/update/pallas_call | solution.py:664
